TPU v7x, 32 devices: a whole 2x2x4 slice. The times are simulated.
32 devices in a mesh: sta: 4 (over y, core), src: 8 (over z, x).
Axes of the slice: x: 2, y: 2, z: 4, core: 2. Of those that a mesh axis runs over, the one named last changes fastest.
Arguments:
- features: bfloat16 [128, 256, 128], P('sta', 'src'), may hold values from -6 to 6
- station_lists: int32 [128, 16], replicated, may hold values from 0 to 127, as said below
- station_counts: int32 [128], replicated, may hold values from 1 to 16
- source_lists: int32 [256, 16], replicated, may hold values from 0 to 255, as said below
- source_counts: int32 [256], replicated, may hold values from 1 to 16
- picks: int32 [2, 128], P(None, 'sta'), may hold values 0 or 1
- targets: float32 [2, 256], P(None, 'src'), may hold values from 0 to 1
- layer_weights: bfloat16 [2, 3, 64, 64], replicated, may hold values from -0.75 to 0.75
- readout_vector: bfloat16 [64], replicated, may hold values from -0.75 to 0.75
Outputs:
- likelihood: float32 [2, 256], P(None, 'src')
- feature_grad: bfloat16 [128, 256, 128], P('sta', 'src')
- weight_grad: float32 [2, 3, 64, 64], replicated
- vector_grad: float32 [64], replicated
Inputs may be any that keep to these rules, and one draw needn't show every extreme that they name: `station_lists`: every entry of a station's list lies within 16 rows of that station; entries past its count are padding. `source_lists`: every entry of a source node's list lies within 16 rows of that source node; entries past its count are padding.
All inputs are finite; a program needn't handle non-finite values. No bound on the sum of `picks` on one device may be relied on, other than what follows from the above.
Results may differ from a plain program's by a relative error of at most 0.015.
Values may be sent and summed in bfloat16 or wider, within the bound.
A program may use at most 64 MiB of HBM per device.

v0:
```python
import jax
import jax.numpy as jnp
from jax import lax
from jax.sharding import PartitionSpec as P

LAYERS = 2
HW = 16


def padded_2(cells, sides, width):
    for axis, dim in sides:
        count = lax.axis_size(axis)
        ends = count - 1
        head = lax.slice_in_dim(cells, 0, width, axis=dim)
        tail = lax.slice_in_dim(cells, cells.shape[dim] - width, cells.shape[dim], axis=dim)
        cells = jnp.concatenate(
            [
                lax.ppermute(tail, axis, [(i, (i + 1) % count) for i in range(ends)]),
                cells,
                lax.ppermute(head, axis, [((i + 1) % count, i) for i in range(ends)]),
            ],
            axis=dim,
        )
    return cells


def count_matrix(lists, counts, first_row, span):
    list_width = lists.shape[1]
    in_list = jnp.arange(list_width)[None, :] < counts[:, None]
    shifted = lists - first_row
    matches = (shifted[:, :, None] == jnp.arange(span)[None, None, :]) & in_list[:, :, None]
    return jnp.sum(matches.astype(jnp.float32), axis=1).astype(jnp.bfloat16)


def blocked(matrix, windows):
    return jnp.kron(jnp.eye(windows, dtype=jnp.bfloat16), matrix)


def apply_block(values, matrix):
    channels = values.shape[-1]
    flat = values.reshape(-1, channels)
    return jnp.dot(flat, matrix, preferred_element_type=jnp.float32).reshape(values.shape)


def outer_sum(left, right, feature):
    return jnp.einsum(
        "nf,ng->fg",
        left.reshape(-1, feature),
        right.reshape(-1, feature),
        preferred_element_type=jnp.float32,
    )


def shards(
    features,
    station_lists,
    station_counts,
    source_lists,
    source_counts,
    picks,
    targets,
    layer_weights,
    readout_vector,
):
    sta_rows, src_rows, channels = features.shape
    feature = layer_weights.shape[-1]
    windows = channels // feature
    sta_first = lax.axis_index("sta") * sta_rows
    src_first = lax.axis_index("src") * src_rows
    own_slists = lax.dynamic_slice_in_dim(station_lists, sta_first, sta_rows, 0)
    own_scounts = lax.dynamic_slice_in_dim(station_counts, sta_first, sta_rows, 0)
    own_rlists = lax.dynamic_slice_in_dim(source_lists, src_first, src_rows, 0)
    own_rcounts = lax.dynamic_slice_in_dim(source_counts, src_first, src_rows, 0)
    sta_mix = count_matrix(own_slists, own_scounts, sta_first - HW, sta_rows + 2 * HW)
    src_mix = count_matrix(own_rlists, own_rcounts, src_first - HW, src_rows + 2 * HW)
    sta_div = own_scounts.astype(jnp.float32)[:, None, None]
    src_div = own_rcounts.astype(jnp.float32)[None, :, None]
    blocks = [
        [blocked(layer_weights[layer_idx, which], windows) for which in range(3)]
        for layer_idx in range(LAYERS)
    ]
    states = features
    saved = []
    for layer_idx in range(LAYERS):
        padded = padded_2(states, (("sta", 0), ("src", 1)), HW)
        along_sta = jnp.einsum(
            "im,mjc->ijc",
            sta_mix,
            padded[:, HW : HW + src_rows],
            preferred_element_type=jnp.float32,
        )
        sta_mean = (along_sta / sta_div).astype(jnp.bfloat16)
        along_src = jnp.einsum(
            "jm,imc->ijc", src_mix, padded[HW : HW + sta_rows], preferred_element_type=jnp.float32
        )
        src_mean = (along_src / src_div).astype(jnp.bfloat16)
        linear = (
            apply_block(states, blocks[layer_idx][0])
            + apply_block(sta_mean, blocks[layer_idx][1])
            + apply_block(src_mean, blocks[layer_idx][2])
        )
        squashed = jnp.tanh(linear)
        saved.append((states, sta_mean, src_mean, squashed))
        states = (states.astype(jnp.float32) + squashed).astype(jnp.bfloat16)
    vector_cols = (
        jnp.eye(windows, dtype=jnp.bfloat16)[:, None, :] * readout_vector[None, :, None]
    ).reshape(channels, windows)
    score = jnp.dot(
        states.reshape(-1, channels), vector_cols, preferred_element_type=jnp.float32
    ).reshape(sta_rows, src_rows, windows)
    picked = picks.astype(jnp.float32)
    partial_sum = jnp.sum(picked.T[:, None, :] * score, axis=0).T
    local_count = jnp.sum(picked, axis=1)
    summed, count = lax.psum((partial_sum, local_count), "sta")
    root = jnp.sqrt(jnp.maximum(count, 1.0))
    likelihood = summed / root[:, None]
    error = jax.nn.sigmoid(likelihood) - targets
    d_score = (picked.T[:, None, :] * error.T[None, :, :]).astype(jnp.bfloat16)
    v_sum = jnp.einsum(
        "nw,nwf->f",
        d_score.reshape(-1, windows),
        states.reshape(-1, windows, feature),
        preferred_element_type=jnp.float32,
    )
    grad = (d_score.astype(jnp.float32)[..., None] * readout_vector.astype(jnp.float32)).reshape(
        sta_rows, src_rows, channels
    )
    w_rows = []
    for layer_idx in reversed(range(LAYERS)):
        before, sta_mean, src_mean, squashed = saved[layer_idx]
        delta = (grad * (1.0 - squashed * squashed)).astype(jnp.bfloat16)
        w_rows.append(
            jnp.stack(
                [
                    outer_sum(before, delta, feature),
                    outer_sum(sta_mean, delta, feature),
                    outer_sum(src_mean, delta, feature),
                ]
            )
        )
        u_sta = (apply_block(delta, blocks[layer_idx][1].T) / sta_div).astype(jnp.bfloat16)
        u_src = (apply_block(delta, blocks[layer_idx][2].T) / src_div).astype(jnp.bfloat16)
        direct = grad + apply_block(delta, blocks[layer_idx][0].T)
        spread_sta = jnp.einsum("im,ijc->mjc", sta_mix, u_sta, preferred_element_type=jnp.float32)
        rim_rows = jnp.concatenate([spread_sta[:HW], spread_sta[sta_rows + HW :]], 0)
        got_rows = padded_2(rim_rows.astype(jnp.bfloat16), (("sta", 0),), HW).astype(rim_rows.dtype)
        from_sta = spread_sta[HW : sta_rows + HW]
        from_sta = from_sta + jnp.pad(got_rows[:HW], ((0, sta_rows - HW), (0, 0), (0, 0)))
        from_sta = from_sta + jnp.pad(got_rows[3 * HW :], ((sta_rows - HW, 0), (0, 0), (0, 0)))
        spread_src = jnp.einsum("jm,ijc->imc", src_mix, u_src, preferred_element_type=jnp.float32)
        rim_cols = jnp.concatenate([spread_src[:, :HW], spread_src[:, src_rows + HW :]], 1)
        got_cols = padded_2(rim_cols.astype(jnp.bfloat16), (("src", 1),), HW).astype(rim_cols.dtype)
        from_src = spread_src[:, HW : src_rows + HW]
        from_src = from_src + jnp.pad(got_cols[:, :HW], ((0, 0), (0, src_rows - HW), (0, 0)))
        from_src = from_src + jnp.pad(got_cols[:, 3 * HW :], ((0, 0), (src_rows - HW, 0), (0, 0)))
        grad = direct + from_sta + from_src
    w_sum = jnp.stack(w_rows[::-1])
    w_total, v_total = lax.psum((w_sum, v_sum), ("sta", "src"))
    node_total = jnp.float32(sta_rows * lax.axis_size("sta")) * jnp.float32(
        src_rows * lax.axis_size("src")
    )
    factor = 1.0 / jnp.sqrt(node_total)
    return (likelihood, grad.astype(jnp.bfloat16), w_total * factor, v_total * factor)


def solution(mesh):
    in_specs = (P("sta", "src", None), P(), P(), P(), P(), P(None, "sta"), P(None, "src"), P(), P())
    out_specs = (P(None, "src"), P("sta", "src", None), P(), P())
    return jax.shard_map(shards, mesh=mesh, in_specs=in_specs, out_specs=out_specs, check_vma=False)
```

profile of v0, /device:TPU:0, one launch (start us, length us, event | category | flops | bytes accessed | tf_op | source)
XLA Modules:
  0.0 294.1 jit_solution(10382133385865042283)
XLA Ops:
  7.2 1.0 fusion.68
  8.3 2.4 collective-permute-start
  10.7 1.3 collective-permute-start.1
  17.6 1.1 reshape.263
  22.6 0.8 convert_reduce_fusion
  23.6 4.2 %collective-permute-start.2 = (bf16[64,16,128]{2,0,1:T(8,128)(2,1)S(1)}, bf16[64,16,128]{2,0,1:T(8,128)(2,1)S(1)}, u32[]{:S(2)}, u32[]{:S(2)}) collective-permute-start(bf16[64,16,128]{2,0,1:T(8,128)(2,1)S(1)} %get-tuple-element.38), channel_id=1, source_target_pairs={{0,1},{1,2},{2,3},{3,4},{4,5},{5,6},{6,7},{8,9},{9,10},{10,11},{11... | collective-permute-start | bytes 786440 | tf_op jit(solution)/shard_map/ppermute | solution.py:18
  27.9 1.3 collective-permute-start.3
  29.5 1.1 reshape.264
  30.6 1.0 convolution_add_fusion.5
  31.6 1.4 collective-permute-done.2
  33.0 4.7 %collective-permute-done.3 = bf16[64,16,128]{2,0,1:T(8,128)(2,1)S(1)} collective-permute-done((bf16[64,16,128]{2,0,1:T(8,128)(2,1)S(1)}, bf16[64,16,128]{2,0,1:T(8,128)(2,1)S(1)}, u32[]{:S(2)}, u32[]{:S(2)}) %collective-permute-start.3) | collective-permute-done | bytes 262176 | tf_op jit(solution)/shard_map/ppermute | solution.py:20
  38.7 1.1 reshape.265
  39.8 1.0 add_convert_fusion.1
  40.8 1.0 reshape.266
  41.9 4.4 %collective-permute-start.4 = (bf16[16,32,128]{2,1,0:T(8,128)(2,1)S(1)}, bf16[16,32,128]{2,1,0:T(8,128)(2,1)S(1)}, u32[]{:S(2)}, u32[]{:S(2)}) collective-permute-start(bf16[16,32,128]{2,1,0:T(8,128)(2,1)S(1)} %get-tuple-element.40), channel_id=1, source_target_pairs={{0,8},{8,16},{16,24},{1,9},{9,17},{17,25},{2,10},{10,18},{18,26},{... | collective-permute-start | bytes 393224 | tf_op jit(solution)/shard_map/ppermute | solution.py:18
  46.3 1.3 collective-permute-start.5
  47.8 3.1 %collective-permute-done.5 = bf16[16,32,128]{2,1,0:T(8,128)(2,1)S(1)} collective-permute-done((bf16[16,32,128]{2,1,0:T(8,128)(2,1)S(1)}, bf16[16,32,128]{2,1,0:T(8,128)(2,1)S(1)}, u32[]{:S(2)}, u32[]{:S(2)}) %collective-permute-start.5) | collective-permute-done | bytes 131104 | tf_op jit(solution)/shard_map/ppermute | solution.py:20
  51.0 4.4 %collective-permute-start.6 = (bf16[64,16,128]{2,1,0:T(8,128)(2,1)S(1)}, bf16[64,16,128]{2,1,0:T(8,128)(2,1)S(1)}, u32[]{:S(2)}, u32[]{:S(2)}) collective-permute-start(bf16[64,16,128]{2,1,0:T(8,128)(2,1)S(1)} %get-tuple-element.36), channel_id=1, source_target_pairs={{0,1},{1,2},{2,3},{3,4},{4,5},{5,6},{6,7},{8,9},{9,10},{10,11},{11... | collective-permute-start | bytes 786440 | tf_op jit(solution)/shard_map/ppermute | solution.py:18
  55.4 1.3 collective-permute-start.7
  57.2 1.1 reshape.268
  58.5 1.0 collective-permute-done.6
  59.5 4.8 %collective-permute-done.7 = bf16[64,16,128]{2,1,0:T(8,128)(2,1)S(1)} collective-permute-done((bf16[64,16,128]{2,1,0:T(8,128)(2,1)S(1)}, bf16[64,16,128]{2,1,0:T(8,128)(2,1)S(1)}, u32[]{:S(2)}, u32[]{:S(2)}) %collective-permute-start.7) | collective-permute-done | bytes 262176 | tf_op jit(solution)/shard_map/ppermute | solution.py:20
  64.5 1.1 reshape.269
  65.8 1.1 reshape.270
  68.1 9.3 %all-reduce.4 = (f32[2,32]{1,0:T(2,128)S(1)}, f32[2]{0:T(128)S(1)}) all-reduce(f32[2,32]{1,0:T(2,128)S(1)} %bitcast.115, f32[2]{0:T(128)S(1)} %copy-done.44), channel_id=1, replica_groups=mesh['sta'=4,'src'=8] {'sta'}, use_global_device_ids=true, to_apply=%region_3.4 | all-reduce | flops 66 | bytes 528 | tf_op jit(solution)/shard_map/psum | solution.py:114
  79.8 1.2 mul.284
  83.5 1.4 copy.149
  85.6 2.4 fusion.69
  88.2 42.1 %psum.31 = f32[64]{0:T(128)S(1)} all-reduce(f32[64]{0:T(128)S(1)} %convolution_bitcast_fusion.9), channel_id=1, replica_groups=mesh['sta'=4,'src'=8] {'sta','src'}, use_global_device_ids=true, to_apply=%region_7.8 | all-reduce | flops 64 | bytes 512 | tf_op jit(solution)/shard_map/psum | solution.py:158
  131.9 0.9 convolution_bitcast_fusion.4
  133.0 1.4 collective-permute-start.8
  134.4 1.3 collective-permute-start.9
  135.8 4.2 %collective-permute-start.10 = (bf16[32,16,128]{2,1,0:T(8,128)(2,1)S(1)}, bf16[32,16,128]{2,1,0:T(8,128)(2,1)S(1)}, u32[]{:S(2)}, u32[]{:S(2)}) collective-permute-start(bf16[32,16,128]{2,1,0:T(8,128)(2,1)S(1)} %get-tuple-element.34), channel_id=1, source_target_pairs={{0,1},{1,2},{2,3},{3,4},{4,5},{5,6},{6,7},{8,9},{9,10},{10,11},{11... | collective-permute-start | bytes 393224 | tf_op jit(solution)/shard_map/ppermute | solution.py:18
  140.0 1.5 collective-permute-start.11
  141.4 0.9 convolution_bitcast_fusion.5
  142.5 4.3 %collective-permute-done.11 = bf16[32,16,128]{2,1,0:T(8,128)(2,1)S(1)} collective-permute-done((bf16[32,16,128]{2,1,0:T(8,128)(2,1)S(1)}, bf16[32,16,128]{2,1,0:T(8,128)(2,1)S(1)}, u32[]{:S(2)}, u32[]{:S(2)}) %collective-permute-start.11) | collective-permute-done | bytes 131104 | tf_op jit(solution)/shard_map/ppermute | solution.py:20
  147.0 0.9 copy-done.8
  147.9 1.2 multiply_convert_fusion
  151.6 1.7 fusion.70
  157.0 3.5 %collective-permute-start.12 = (bf16[16,32,128]{2,1,0:T(8,128)(2,1)S(1)}, bf16[16,32,128]{2,1,0:T(8,128)(2,1)S(1)}, u32[]{:S(2)}, u32[]{:S(2)}) collective-permute-start(bf16[16,32,128]{2,1,0:T(8,128)(2,1)S(1)} %get-tuple-element.28), channel_id=1, source_target_pairs={{0,8},{8,16},{16,24},{1,9},{9,17},{17,25},{2,10},{10,18},{18,26},{... | collective-permute-start | bytes 393224 | tf_op jit(solution)/shard_map/ppermute | solution.py:18
  160.5 1.3 collective-permute-start.13
  161.8 4.1 %collective-permute-start.14 = (bf16[32,16,128]{2,1,0:T(8,128)(2,1)S(1)}, bf16[32,16,128]{2,1,0:T(8,128)(2,1)S(1)}, u32[]{:S(2)}, u32[]{:S(2)}) collective-permute-start(bf16[32,16,128]{2,1,0:T(8,128)(2,1)S(1)} %get-tuple-element.30), channel_id=1, source_target_pairs={{0,1},{1,2},{2,3},{3,4},{4,5},{5,6},{6,7},{8,9},{9,10},{10,11},{11... | collective-permute-start | bytes 393224 | tf_op jit(solution)/shard_map/ppermute | solution.py:18
  165.9 1.3 collective-permute-start.15
  167.2 115.8 %all-reduce.7.cloned.1.call-done = f32[2,3,64,64]{2,3,1,0:T(8,128)} async-done(((f32[2,3,64,64]{2,3,1,0:T(8,128)}), f32[2,3,64,64]{2,3,1,0:T(8,128)}) %all-reduce.7.cloned.1.call-update) | async-done | bytes 98320 | tf_op jit(solution)/shard_map/psum | solution.py:158
  283.0 0.9 broadcast_multiply_fusion
  283.9 0.8 copy.116
  285.1 1.0 copy-done.11
  286.2 1.0 fusion.17
  (185 shorter events, 27.9 us)
Async XLA Ops:
  7.2 275.8 %all-reduce.7.cloned.1.call-start = ((), (), s32[]{:S(2)}) async-start(), calls=%async_computation | async-start | bytes 393216 | tf_op jit(solution)/shard_map/psum | solution.py:158
  8.3 15.1 %collective-permute-start = (bf16[16,32,128]{2,0,1:T(8,128)(2,1)S(1)}, bf16[16,32,128]{2,0,1:T(8,128)(2,1)S(1)}, u32[]{:S(2)}, u32[]{:S(2)}) collective-permute-start(bf16[16,32,128]{2,0,1:T(8,128)(2,1)S(1)} %copy.146), channel_id=1, source_target_pairs={{0,8},{8,16},{16,24},{1,9},{9,17},{17,25},{2,10},{10,18},{18,26},{... | collective-permute-start | bytes 393224 | tf_op jit(solution)/shard_map/ppermute | solution.py:18
  10.6 4.4 %copy-start.19 = (bf16[2,3,64,64]{3,2,1,0:T(8,128)(2,1)S(1)}, bf16[2,3,64,64]{3,2,1,0:T(8,128)(2,1)}, u32[]{:S(2)}) copy-start(bf16[2,3,64,64]{3,2,1,0:T(8,128)(2,1)} %param.16) | copy-start | bytes 147460
  10.7 12.8 %collective-permute-start.1 = (bf16[16,32,128]{2,0,1:T(8,128)(2,1)S(1)}, bf16[16,32,128]{2,0,1:T(8,128)(2,1)S(1)}, u32[]{:S(2)}, u32[]{:S(2)}) collective-permute-start(bf16[16,32,128]{2,0,1:T(8,128)(2,1)S(1)} %copy.147), channel_id=1, source_target_pairs={{8,0},{16,8},{24,16},{9,1},{17,9},{25,17},{10,2},{18,10},{26,18},{... | collective-permute-start | bytes 393224 | tf_op jit(solution)/shard_map/ppermute | solution.py:20
  12.7 1.4 copy-start.36
  12.7 54.6 %copy-start.20 = (f32[32,2]{0,1:T(2,128)}, f32[32,2]{0,1:T(2,128)S(1)}, u32[]{:S(2)}) copy-start(f32[32,2]{0,1:T(2,128)S(1)} %convert_bitcast_fusion) | copy-start | bytes 772
  14.1 0.8 copy-start.28
  15.0 1.4 copy-start
  16.5 40.3 %copy-start.22 = (bf16[32,64]{1,0:T(8,128)(2,1)}, bf16[32,64]{1,0:T(8,128)(2,1)S(1)}, u32[]{:S(2)}) copy-start(bf16[32,64]{1,0:T(8,128)(2,1)S(1)} %convert_reduce_fusion.1) | copy-start | bytes 12292
  23.6 9.4 %collective-permute-start.2 = (bf16[64,16,128]{2,0,1:T(8,128)(2,1)S(1)}, bf16[64,16,128]{2,0,1:T(8,128)(2,1)S(1)}, u32[]{:S(2)}, u32[]{:S(2)}) collective-permute-start(bf16[64,16,128]{2,0,1:T(8,128)(2,1)S(1)} %get-tuple-element.38), channel_id=1, source_target_pairs={{0,1},{1,2},{2,3},{3,4},{4,5},{5,6},{6,7},{8,9},{9,10},{10,11},{11... | collective-permute-start | bytes 786440 | tf_op jit(solution)/shard_map/ppermute | solution.py:18
  27.9 1.3 copy-start.39
  27.9 9.9 %collective-permute-start.3 = (bf16[64,16,128]{2,0,1:T(8,128)(2,1)S(1)}, bf16[64,16,128]{2,0,1:T(8,128)(2,1)S(1)}, u32[]{:S(2)}, u32[]{:S(2)}) collective-permute-start(bf16[64,16,128]{2,0,1:T(8,128)(2,1)S(1)} %get-tuple-element.39), channel_id=1, source_target_pairs={{1,0},{2,1},{3,2},{4,3},{5,4},{6,5},{7,6},{9,8},{10,9},{11,10},{12... | collective-permute-start | bytes 786440 | tf_op jit(solution)/shard_map/ppermute | solution.py:20
  31.6 6.2 %copy-start.25 = (bf16[32,64]{1,0:T(8,128)(2,1)S(1)}, bf16[32,64]{1,0:T(8,128)(2,1)}, u32[]{:S(2)}) copy-start(bf16[32,64]{1,0:T(8,128)(2,1)} %convert_reduce_fusion) | copy-start | bytes 12292
  41.9 5.9 %collective-permute-start.4 = (bf16[16,32,128]{2,1,0:T(8,128)(2,1)S(1)}, bf16[16,32,128]{2,1,0:T(8,128)(2,1)S(1)}, u32[]{:S(2)}, u32[]{:S(2)}) collective-permute-start(bf16[16,32,128]{2,1,0:T(8,128)(2,1)S(1)} %get-tuple-element.40), channel_id=1, source_target_pairs={{0,8},{8,16},{16,24},{1,9},{9,17},{17,25},{2,10},{10,18},{18,26},{... | collective-permute-start | bytes 393224 | tf_op jit(solution)/shard_map/ppermute | solution.py:18
  46.3 4.6 %collective-permute-start.5 = (bf16[16,32,128]{2,1,0:T(8,128)(2,1)S(1)}, bf16[16,32,128]{2,1,0:T(8,128)(2,1)S(1)}, u32[]{:S(2)}, u32[]{:S(2)}) collective-permute-start(bf16[16,32,128]{2,1,0:T(8,128)(2,1)S(1)} %get-tuple-element.41), channel_id=1, source_target_pairs={{8,0},{16,8},{24,16},{9,1},{17,9},{25,17},{10,2},{18,10},{26,18},{... | collective-permute-start | bytes 393224 | tf_op jit(solution)/shard_map/ppermute | solution.py:20
  51.0 5.7 %copy-start.40 = (f32[32]{0:T(128)S(1)}, f32[32]{0:T(128)}, u32[]{:S(2)}) copy-start(f32[32]{0:T(128)} %get-tuple-element.26) | copy-start | bytes 388
  51.0 8.4 %collective-permute-start.6 = (bf16[64,16,128]{2,1,0:T(8,128)(2,1)S(1)}, bf16[64,16,128]{2,1,0:T(8,128)(2,1)S(1)}, u32[]{:S(2)}, u32[]{:S(2)}) collective-permute-start(bf16[64,16,128]{2,1,0:T(8,128)(2,1)S(1)} %get-tuple-element.36), channel_id=1, source_target_pairs={{0,1},{1,2},{2,3},{3,4},{4,5},{5,6},{6,7},{8,9},{9,10},{10,11},{11... | collective-permute-start | bytes 786440 | tf_op jit(solution)/shard_map/ppermute | solution.py:18
  55.4 8.8 %collective-permute-start.7 = (bf16[64,16,128]{2,1,0:T(8,128)(2,1)S(1)}, bf16[64,16,128]{2,1,0:T(8,128)(2,1)S(1)}, u32[]{:S(2)}, u32[]{:S(2)}) collective-permute-start(bf16[64,16,128]{2,1,0:T(8,128)(2,1)S(1)} %get-tuple-element.37), channel_id=1, source_target_pairs={{1,0},{2,1},{3,2},{4,3},{5,4},{6,5},{7,6},{9,8},{10,9},{11,10},{12... | collective-permute-start | bytes 786440 | tf_op jit(solution)/shard_map/ppermute | solution.py:20
  57.2 1.1 copy-start.18
  58.2 6.0 %copy-start.26 = (bf16[32,64]{1,0:T(8,128)(2,1)S(1)}, bf16[32,64]{1,0:T(8,128)(2,1)}, u32[]{:S(2)}) copy-start(bf16[32,64]{1,0:T(8,128)(2,1)} %convert_reduce_fusion) | copy-start | bytes 12292
  65.8 1.1 copy-start.35
  85.6 2.5 copy-start.1
  88.0 42.9 %copy-start.7 = (bf16[2048,64]{1,0:T(8,128)(2,1)S(1)}, bf16[2048,64]{1,0:T(8,128)(2,1)}, u32[]{:S(2)}) copy-start(bf16[2048,64]{1,0:T(8,128)(2,1)} %reshape.269) | copy-start | bytes 786436
  130.9 1.0 copy-start.6
  131.9 1.0 copy-start.10
  131.9 3.8 %copy-start.16 = (bf16[32,64,128]{2,1,0:T(8,128)(2,1)S(1)}, bf16[32,64,128]{2,1,0:T(8,128)(2,1)}, u32[]{:S(2)}) copy-start(bf16[32,64,128]{2,1,0:T(8,128)(2,1)} %get-tuple-element.62) | copy-start | bytes 1572868
  133.0 8.5 %copy-start.5 = (bf16[2048,64]{1,0:T(8,128)(2,1)S(1)}, bf16[2048,64]{1,0:T(8,128)(2,1)}, u32[]{:S(2)}) copy-start(bf16[2048,64]{1,0:T(8,128)(2,1)} %reshape.266) | copy-start | bytes 786436
  133.0 9.4 %collective-permute-start.8 = (bf16[16,32,128]{2,1,0:T(8,128)(2,1)S(1)}, bf16[16,32,128]{2,1,0:T(8,128)(2,1)S(1)}, u32[]{:S(2)}, u32[]{:S(2)}) collective-permute-start(bf16[16,32,128]{2,1,0:T(8,128)(2,1)S(1)} %get-tuple-element.32), channel_id=1, source_target_pairs={{0,8},{8,16},{16,24},{1,9},{9,17},{17,25},{2,10},{10,18},{18,26},{... | collective-permute-start | bytes 393224 | tf_op jit(solution)/shard_map/ppermute | solution.py:18
  134.4 8.0 %collective-permute-start.9 = (bf16[16,32,128]{2,1,0:T(8,128)(2,1)S(1)}, bf16[16,32,128]{2,1,0:T(8,128)(2,1)S(1)}, u32[]{:S(2)}, u32[]{:S(2)}) collective-permute-start(bf16[16,32,128]{2,1,0:T(8,128)(2,1)S(1)} %get-tuple-element.33), channel_id=1, source_target_pairs={{8,0},{16,8},{24,16},{9,1},{17,9},{25,17},{10,2},{18,10},{26,18},{... | collective-permute-start | bytes 393224 | tf_op jit(solution)/shard_map/ppermute | solution.py:20
  135.8 6.8 %collective-permute-start.10 = (bf16[32,16,128]{2,1,0:T(8,128)(2,1)S(1)}, bf16[32,16,128]{2,1,0:T(8,128)(2,1)S(1)}, u32[]{:S(2)}, u32[]{:S(2)}) collective-permute-start(bf16[32,16,128]{2,1,0:T(8,128)(2,1)S(1)} %get-tuple-element.34), channel_id=1, source_target_pairs={{0,1},{1,2},{2,3},{3,4},{4,5},{5,6},{6,7},{8,9},{9,10},{10,11},{11... | collective-permute-start | bytes 393224 | tf_op jit(solution)/shard_map/ppermute | solution.py:18
  140.0 6.9 %collective-permute-start.11 = (bf16[32,16,128]{2,1,0:T(8,128)(2,1)S(1)}, bf16[32,16,128]{2,1,0:T(8,128)(2,1)S(1)}, u32[]{:S(2)}, u32[]{:S(2)}) collective-permute-start(bf16[32,16,128]{2,1,0:T(8,128)(2,1)S(1)} %get-tuple-element.35), channel_id=1, source_target_pairs={{1,0},{2,1},{3,2},{4,3},{5,4},{6,5},{7,6},{9,8},{10,9},{11,10},{12... | collective-permute-start | bytes 393224 | tf_op jit(solution)/shard_map/ppermute | solution.py:20
  142.5 4.5 %copy-start.12 = (f32[32,64,128]{2,1,0:T(8,128)S(1)}, f32[32,64,128]{2,1,0:T(8,128)}, u32[]{:S(2)}) copy-start(f32[32,64,128]{2,1,0:T(8,128)} %get-tuple-element.63) | copy-start | bytes 3145732
  146.8 1.0 copy-start.8
  147.0 0.9 copy-start.29
  147.0 0.9 copy-start.32
  149.1 0.8 copy-start.24
  149.1 0.8 copy-start.41
  151.6 1.7 copy-start.4
  153.4 1.0 copy-start.3
  154.4 1.0 copy-start.2
  155.4 0.8 copy-start.14
  156.2 5.5 %copy-start.15 = (bf16[32,64,128]{2,1,0:T(8,128)(2,1)S(1)}, bf16[32,64,128]{2,1,0:T(8,128)(2,1)}, u32[]{:S(2)}) copy-start(bf16[32,64,128]{2,1,0:T(8,128)(2,1)} %get-tuple-element.66) | copy-start | bytes 1572868
  157.0 127.8 %collective-permute-start.12 = (bf16[16,32,128]{2,1,0:T(8,128)(2,1)S(1)}, bf16[16,32,128]{2,1,0:T(8,128)(2,1)S(1)}, u32[]{:S(2)}, u32[]{:S(2)}) collective-permute-start(bf16[16,32,128]{2,1,0:T(8,128)(2,1)S(1)} %get-tuple-element.28), channel_id=1, source_target_pairs={{0,8},{8,16},{16,24},{1,9},{9,17},{17,25},{2,10},{10,18},{18,26},{... | collective-permute-start | bytes 393224 | tf_op jit(solution)/shard_map/ppermute | solution.py:18
  160.5 124.3 %collective-permute-start.13 = (bf16[16,32,128]{2,1,0:T(8,128)(2,1)S(1)}, bf16[16,32,128]{2,1,0:T(8,128)(2,1)S(1)}, u32[]{:S(2)}, u32[]{:S(2)}) collective-permute-start(bf16[16,32,128]{2,1,0:T(8,128)(2,1)S(1)} %get-tuple-element.29), channel_id=1, source_target_pairs={{8,0},{16,8},{24,16},{9,1},{17,9},{25,17},{10,2},{18,10},{26,18},{... | collective-permute-start | bytes 393224 | tf_op jit(solution)/shard_map/ppermute | solution.py:20
  161.8 123.1 %collective-permute-start.14 = (bf16[32,16,128]{2,1,0:T(8,128)(2,1)S(1)}, bf16[32,16,128]{2,1,0:T(8,128)(2,1)S(1)}, u32[]{:S(2)}, u32[]{:S(2)}) collective-permute-start(bf16[32,16,128]{2,1,0:T(8,128)(2,1)S(1)} %get-tuple-element.30), channel_id=1, source_target_pairs={{0,1},{1,2},{2,3},{3,4},{4,5},{5,6},{6,7},{8,9},{9,10},{10,11},{11... | collective-permute-start | bytes 393224 | tf_op jit(solution)/shard_map/ppermute | solution.py:18
  165.9 119.0 %collective-permute-start.15 = (bf16[32,16,128]{2,1,0:T(8,128)(2,1)S(1)}, bf16[32,16,128]{2,1,0:T(8,128)(2,1)S(1)}, u32[]{:S(2)}, u32[]{:S(2)}) collective-permute-start(bf16[32,16,128]{2,1,0:T(8,128)(2,1)S(1)} %get-tuple-element.31), channel_id=1, source_target_pairs={{1,0},{2,1},{3,2},{4,3},{5,4},{6,5},{7,6},{9,8},{10,9},{11,10},{12... | collective-permute-start | bytes 393224 | tf_op jit(solution)/shard_map/ppermute | solution.py:20
  284.9 1.2 copy-start.11
  284.9 1.3 copy-start.9
  (14 other events, 9.7 us)
Sparse Core Ops, SparseCore 0:
  157.1 125.8 all-reduce.6
where the time goes:
time: 296 us; the launch traced here: 294 us
  waiting for transfers between devices  135 us (46%)
  blocking collectives  51.4 us (17%)
  starting transfers between devices  39.2 us (13%)
  local copies, waits for them, and re-layouts  31.2 us (11%)
  matrix products  14.9 us (5%)
  between operations  14.9 us (5%)
  other arithmetic  7.36 us (2%)
    psum x1, waiting for transfers between devices, shards(): w_total, v_total = lax.psum((w_sum, v_sum), ('sta', 'src'))  116 us
    psum x1, blocking collectives, shards(): w_total, v_total = lax.psum((w_sum, v_sum), ('sta', 'src'))  42.1 us
    ppermute x8, starting transfers between devices, padded_2(): lax.ppermute(tail, axis, [(i, (i + 1) % count) for i in range(ends)])  28.6 us
    ppermute x8, waiting for transfers between devices, padded_2(): lax.ppermute(head, axis, [((i + 1) % count, i) for i in range(ends)])  16.9 us
    unnamed x95, local copies, waits for them, and re-layouts  12.8 us
    ppermute x8, starting transfers between devices, padded_2(): lax.ppermute(head, axis, [((i + 1) % count, i) for i in range(ends)])  10.5 us
    psum x1, blocking collectives, shards(): summed, count = lax.psum((partial_sum, local_count), 'sta')  9.3 us
    reshape x6, local copies, waits for them, and re-layouts, outer_sum(): left.reshape(-1, feature)  6.35 us
  transfers between devices with their start and end apart: 17, of which 7 were waited for; matrix products, arithmetic and copies ran while one was open for 5% of the time, Pallas kernels for 0%

commit v1 on v0

v1 whole, which is shorter than its diff:
```python
import functools

import jax
import jax.numpy as jnp
from jax import lax
from jax.experimental import pallas as pl
from jax.experimental.pallas import tpu as pltpu
from jax.sharding import PartitionSpec as P

LAYERS = 2
HW = 16
J = 16
G = 4
MESH = pl.DeviceIdType.MESH
F32, BF16 = jnp.float32, jnp.bfloat16


def iota(shape, dim):
    return lax.broadcasted_iota(jnp.int32, shape, dim)


def ones_where(cond):
    return jnp.where(cond, 1.0, 0.0).astype(BF16)


def dot(a, b):
    return lax.dot_general(a, b, (((1,), (0,)), ((), ())), preferred_element_type=F32)


def dot_nt(a, b):
    return lax.dot_general(a, b, (((1,), (1,)), ((), ())), preferred_element_type=F32)


def dot_tn(a, b):
    return lax.dot_general(a, b, (((0,), (0,)), ((), ())), preferred_element_type=F32)


def coefs(list_ref, count_row, start, rows, base, span):
    start = pl.multiple_of(start, HW)
    lists = list_ref[pl.ds(start, rows), :] - base
    lanes = iota((rows, count_row.shape[1]), 1)
    own = iota((rows, count_row.shape[1]), 0) + start
    count = jnp.sum(jnp.where(lanes == own, count_row, 0.0), axis=1, keepdims=True)
    place = iota((rows, span), 1)
    total = jnp.zeros((rows, span), F32)
    for k in range(lists.shape[1]):
        hit = (lists[:, k : k + 1] == place) & (count > float(k))
        total = total + jnp.where(hit, 1.0, 0.0)
    return (total / count).astype(BF16)


def halo_coefs(list_ref, count_row, first, rows, total_rows):
    before = lax.rem(first + total_rows - HW, total_rows)
    after = lax.rem(first + rows, total_rows)
    return jnp.concatenate(
        [
            coefs(list_ref, count_row, before, HW, first, rows),
            coefs(list_ref, count_row, first, rows, first, rows),
            coefs(list_ref, count_row, after, HW, first, rows),
        ],
        axis=0,
    )


def kernel(
    n_sta,
    n_src,
    chunk,
    feat,
    slist,
    scnt,
    rlist,
    rcnt,
    picks,
    targets,
    weights,
    readout,
    lik_out,
    grad_out,
    w_out,
    hs,
    hr,
    x,
    xb,
    slope,
    ks,
    bd,
    wf,
    q,
    qt,
    lik_slots,
    w_local,
    sta_slots,
    src_slots,
    total,
    halo_send,
    halo_recv,
    lik_send,
    lik_recv,
    a_send,
    a_recv,
    b_send,
    b_recv,
    c_send,
    c_recv,
):
    me_sta = lax.axis_index("sta")
    me_src = lax.axis_index("src")
    rows, cols, lanes = feat.shape
    feature = weights.shape[-1]
    windows = lanes // feature
    span_s, span_r = rows + 2 * HW, cols + 2 * HW
    nodes = rows * cols
    sta_first, src_first = me_sta * rows, me_src * cols

    def sta_peer(d):
        return lax.rem(me_sta + d, n_sta)

    def src_peer(d):
        return lax.rem(me_src + d, n_src)

    for e in range(2 * LAYERS):
        zero_s = jnp.zeros((HW, cols, lanes), BF16)
        zero_r = jnp.zeros((rows, HW, lanes), BF16)

        @pl.when(me_sta == 0)
        def _():
            hs[e, 0:HW] = zero_s

        @pl.when(me_sta == n_sta - 1)
        def _():
            hs[e, HW + rows :] = zero_s

        @pl.when(me_src == 0)
        def _():
            hr[e, :, 0:HW] = zero_r

        @pl.when(me_src == n_src - 1)
        def _():
            hr[e, :, HW + cols :] = zero_r

    barrier = pltpu.get_barrier_semaphore()
    for d in range(1, n_sta):
        pl.semaphore_signal(barrier, inc=1, device_id={"sta": sta_peer(d)}, device_id_type=MESH)
    for d in range(1, n_src):
        pl.semaphore_signal(barrier, inc=1, device_id={"src": src_peer(d)}, device_id_type=MESH)
    pl.semaphore_wait(barrier, n_sta + n_src - 2)

    def halo_copy(e, direction):
        if direction == 0:
            src, dst, device = hs.at[e, HW : 2 * HW], hs.at[e, HW + rows :], {"sta": me_sta - 1}
        elif direction == 1:
            src, dst, device = hs.at[e, rows : HW + rows], hs.at[e, 0:HW], {"sta": me_sta + 1}
        elif direction == 2:
            src, dst, device = hr.at[e, :, HW : 2 * HW], hr.at[e, :, HW + cols :], {"src": me_src - 1}
        else:
            src, dst, device = hr.at[e, :, cols : HW + cols], hr.at[e, :, 0:HW], {"src": me_src + 1}
        return pltpu.make_async_remote_copy(
            src_ref=src,
            dst_ref=dst,
            send_sem=halo_send.at[e, direction],
            recv_sem=halo_recv.at[e, direction],
            device_id=device,
            device_id_type=MESH,
        )

    has = [me_sta > 0, me_sta < n_sta - 1, me_src > 0, me_src < n_src - 1]

    def halo_start(e, values):
        hr[e, :, HW : HW + cols] = values
        for direction in (2, 3):
            pl.when(has[direction])(lambda: halo_copy(e, direction).start())
        hs[e, HW : HW + rows] = values
        for direction in (0, 1):
            pl.when(has[direction])(lambda: halo_copy(e, direction).start())

    def halo_wait(e, directions):
        for direction in directions:
            pl.when(has[direction ^ 1])(lambda: halo_copy(e, direction).wait_recv())

    def halo_drain(e):
        for direction in range(4):
            pl.when(has[direction])(lambda: halo_copy(e, direction).wait_send())

    states = feat[...]
    halo_start(0, states)

    s_row, r_row = scnt[...].astype(F32), rcnt[...].astype(F32)
    up_rows = ones_where((iota((rows * J, rows), 0) // J) == iota((rows * J, rows), 1))
    up_cols = ones_where((iota((span_s, span_s * J), 1) // J) == iota((span_s, span_s * J), 0))
    rep_rows = ones_where((iota((G * cols, cols), 0) % cols) == iota((G * cols, cols), 1))
    rep_cols = ones_where((iota((span_r, G * span_r), 1) % span_r) == iota((span_r, G * span_r), 0))
    same_col = (iota((rows * J, span_s * J), 0) % J) == (iota((rows * J, span_s * J), 1) % J)
    same_grp = (iota((G * cols, G * span_r), 0) // cols) == (iota((G * cols, G * span_r), 1) // span_r)

    def put_mixes(way, sta_part, src_part):
        wide = dot(sta_part.astype(BF16), up_cols)
        ks[way] = jnp.where(same_col, wide, 0.0).astype(BF16)
        wide = dot(src_part.astype(BF16), rep_cols)
        bd[way] = jnp.where(same_grp, wide, 0.0).astype(BF16)

    fwd_s = coefs(slist, s_row, sta_first, rows, sta_first - HW, span_s)
    fwd_r = coefs(rlist, r_row, src_first, cols, src_first - HW, span_r)
    put_mixes(0, dot(up_rows, fwd_s), dot(rep_rows, fwd_r))

    spread = ones_where((iota((lanes, feature), 0) % feature) == iota((lanes, feature), 1))
    same_win = (iota((lanes, lanes), 0) // feature) == (iota((lanes, lanes), 1) // feature)

    def put_weights(way):
        for l in range(LAYERS):
            for p in range(3):
                m = weights[l, p]
                left = (dot(spread, m) if way == 0 else dot_nt(spread, m)).astype(BF16)
                wide = jnp.where(same_win, dot_nt(left, spread), 0.0)
                wf[way, l, p * lanes : (p + 1) * lanes, :] = wide.astype(BF16)

    put_weights(0)

    def mix_sta(way, e, out):
        for half in range(cols // J):
            part = hs[e, :, half * J : (half + 1) * J, :].reshape(span_s * J, lanes)
            mixed = dot(ks[way], part).astype(BF16)
            out[:, half * J : (half + 1) * J, lanes : 2 * lanes] = mixed.reshape(rows, J, lanes)

    def mix_src(way, e, out):
        for g in range(rows // G):
            part = hr[e, g * G : (g + 1) * G].reshape(G * span_r, lanes)
            mixed = dot(bd[way], part).astype(BF16)
            out[g * G : (g + 1) * G, :, 2 * lanes :] = mixed.reshape(G, cols, lanes)

    wide_readout = dot_nt(readout[...], spread)
    jw = windows * cols
    node_own = iota((jw, lanes), 0)
    win_mask = (node_own // cols) == (iota((jw, lanes), 1) // feature)
    diag = (node_own % cols) == iota((jw, lanes), 1)

    def to_column(row_of):
        wide = jnp.concatenate(
            [jnp.broadcast_to(row_of(w), (cols, lanes)) for w in range(windows)], axis=0
        )
        return jnp.sum(jnp.where(diag, wide, 0.0), axis=1, keepdims=True)

    for l in range(LAYERS):
        x[l, :, :, 0:lanes] = states
        if l == 1:
            t = halo_coefs(slist, s_row, sta_first, rows, n_sta * rows)
            u = halo_coefs(rlist, r_row, src_first, cols, n_src * cols)
            put_mixes(1, dot_nt(up_rows, t), dot_nt(rep_rows, u))
            put_weights(1)
            picked = picks[...].astype(F32)
            wide_picks = jnp.concatenate(
                [jnp.broadcast_to(picked[w : w + 1], (cols, rows)) for w in range(windows)], axis=0
            ).astype(BF16)
            sel = ones_where((iota((nodes, rows), 0) // cols) == iota((nodes, rows), 1))
            at_q = (iota((jw, nodes), 0) % cols) == (iota((jw, nodes), 1) % cols)
            q[...] = jnp.where(at_q, dot_nt(wide_picks, sel), 0.0).astype(BF16)
            at_t = (iota((nodes, jw), 0) % cols) == (iota((nodes, jw), 1) % cols)
            qt[...] = jnp.where(at_t, dot_nt(sel, wide_picks), 0.0).astype(BF16)
        halo_wait(l, (0, 1))
        mix_sta(0, l, x.at[l])
        halo_wait(l, (2, 3))
        mix_src(0, l, x.at[l])
        z = dot(x[l].reshape(nodes, 3 * lanes), wf[0, l])
        squashed = jnp.tanh(z)
        slope[l] = 1.0 - squashed * squashed
        states = (states.astype(F32) + squashed.reshape(rows, cols, lanes)).astype(BF16)
        if l + 1 < LAYERS:
            halo_start(l + 1, states)

    heap = dot(q[...], states.reshape(nodes, lanes))
    score = jnp.sum(jnp.where(win_mask, heap * wide_readout, 0.0), axis=1, keepdims=True)
    flat = jnp.where(diag, score, 0.0)
    tile_row = iota((8, lanes), 0)
    tile = jnp.zeros((8, lanes), F32)
    for w in range(windows):
        part = jnp.sum(flat[w * cols : (w + 1) * cols], axis=0, keepdims=True)
        tile = jnp.where(tile_row == w, part, tile)
        count = jnp.sum(picked[w : w + 1], axis=1, keepdims=True)
        tile = jnp.where(tile_row == windows + w, count, tile)
    lik_slots[me_sta] = tile
    sends = []
    for d in range(1, n_sta):
        sends.append(
            pltpu.make_async_remote_copy(
                src_ref=lik_slots.at[me_sta],
                dst_ref=lik_slots.at[me_sta],
                send_sem=lik_send.at[d],
                recv_sem=lik_recv.at[d],
                device_id={"sta": sta_peer(d)},
                device_id_type=MESH,
            )
        )
        sends[-1].start()
    for copy in sends:
        copy.wait_recv()
    summed = lik_slots[0]
    for s in range(1, n_sta):
        summed = summed + lik_slots[s]
    root = jnp.sqrt(jnp.maximum(summed[windows : 2 * windows], 1.0))
    lik = summed[0:windows] / root
    lik_out[...] = lik[:, :cols]
    sig = jax.nn.sigmoid(lik)
    sig_col = to_column(lambda w: sig[w : w + 1])
    want = jnp.concatenate(
        [jnp.broadcast_to(targets[w : w + 1, :], (cols, cols)) for w in range(windows)], axis=0
    )
    diag_cols = (iota((jw, cols), 0) % cols) == iota((jw, cols), 1)
    want_col = jnp.sum(jnp.where(diag_cols, want, 0.0), axis=1, keepdims=True)
    err = (sig_col - want_col).astype(BF16).astype(F32)
    err_wide = jnp.where(win_mask, err, 0.0)
    v_row = jnp.sum(err_wide * heap, axis=0, keepdims=True)
    grad = dot(qt[...], err_wide.astype(BF16)) * wide_readout

    low = iota((feature, lanes), 1) < feature

    for l in reversed(range(LAYERS)):
        e = 2 * LAYERS - 1 - l
        delta = (grad * slope[l]).astype(BF16)
        delta3 = delta.reshape(rows, cols, lanes)
        halo_start(e, delta3)
        xb[:, :, 0:lanes] = delta3
        w_t = dot_tn(delta, x[l].reshape(nodes, 3 * lanes))
        folded = []
        for p in range(3):
            both = jnp.where(
                low,
                w_t[0:feature, p * lanes : (p + 1) * lanes],
                w_t[feature:, p * lanes : (p + 1) * lanes],
            )
            folded.append(both + pltpu.roll(both, feature, 1))
        w_local[l * feature : (l + 1) * feature] = jnp.where(low, folded[0], folded[1])
        if l == 1:
            kept = folded[2]
        else:
            w_local[2 * feature : 3 * feature] = jnp.where(low, folded[2], kept)
            w_local[3 * feature :] = jnp.broadcast_to(v_row, (w_local.shape[0] - 3 * feature, lanes))
        halo_wait(e, (0, 1))
        mix_sta(1, e, xb)
        halo_wait(e, (2, 3))
        mix_src(1, e, xb)
        grad = grad + dot(xb[...].reshape(nodes, 3 * lanes), wf[1, l])
    grad_out[...] = grad.reshape(rows, cols, lanes).astype(BF16)

    def part(ref, s):
        return ref.at[pl.ds(pl.multiple_of(s * chunk, 8), chunk)]

    first = []
    for d in range(1, n_sta):
        first.append(
            pltpu.make_async_remote_copy(
                src_ref=part(w_local, sta_peer(d)),
                dst_ref=sta_slots.at[me_sta],
                send_sem=a_send.at[d],
                recv_sem=a_recv.at[d],
                device_id={"sta": sta_peer(d)},
                device_id_type=MESH,
            )
        )
        first[-1].start()
    sta_slots[me_sta] = part(w_local, me_sta)[...]
    for copy in first:
        copy.wait_recv()
    some = sta_slots[0]
    for s in range(1, n_sta):
        some = some + sta_slots[s]
    src_slots[me_src] = some
    second = []
    for d in range(1, n_src):
        second.append(
            pltpu.make_async_remote_copy(
                src_ref=src_slots.at[me_src],
                dst_ref=src_slots.at[me_src],
                send_sem=b_send.at[d],
                recv_sem=b_recv.at[d],
                device_id={"src": src_peer(d)},
                device_id_type=MESH,
            )
        )
        second[-1].start()
    for copy in second:
        copy.wait_recv()
    some = src_slots[0]
    for s in range(1, n_src):
        some = some + src_slots[s]
    part(total, me_sta)[...] = some
    third = []
    for d in range(1, n_sta):
        third.append(
            pltpu.make_async_remote_copy(
                src_ref=part(total, me_sta),
                dst_ref=part(total, me_sta),
                send_sem=c_send.at[d],
                recv_sem=c_recv.at[d],
                device_id={"sta": sta_peer(d)},
                device_id_type=MESH,
            )
        )
        third[-1].start()
    for e in range(2 * LAYERS):
        halo_drain(e)
    for copy in third:
        copy.wait_recv()
    w_out[...] = total[...]
    for copy in sends + first + second + third:
        copy.wait_send()


def shards(
    n_sta,
    n_src,
    features,
    station_lists,
    station_counts,
    source_lists,
    source_counts,
    picks,
    targets,
    layer_weights,
    readout_vector,
):
    rows, cols, lanes = features.shape
    feature = layer_weights.shape[-1]
    windows = lanes // feature
    nodes = rows * cols
    span_s, span_r = rows + 2 * HW, cols + 2 * HW
    chunk = -(-(3 * feature + 1) // (8 * n_sta)) * 8
    w_rows = chunk * n_sta
    jw = windows * cols
    dma = pltpu.SemaphoreType.DMA
    vmem = pl.BlockSpec(memory_space=pltpu.VMEM)
    lik, grad, w_sum = pl.pallas_call(
        functools.partial(kernel, n_sta, n_src, chunk),
        out_shape=(
            jax.ShapeDtypeStruct((windows, cols), F32),
            jax.ShapeDtypeStruct((rows, cols, lanes), BF16),
            jax.ShapeDtypeStruct((w_rows, lanes), F32),
        ),
        in_specs=[vmem] * 9,
        out_specs=(vmem,) * 3,
        scratch_shapes=[
            pltpu.VMEM((2 * LAYERS, span_s, cols, lanes), BF16),
            pltpu.VMEM((2 * LAYERS, rows, span_r, lanes), BF16),
            pltpu.VMEM((LAYERS, rows, cols, 3 * lanes), BF16),
            pltpu.VMEM((rows, cols, 3 * lanes), BF16),
            pltpu.VMEM((LAYERS, nodes, lanes), F32),
            pltpu.VMEM((2, rows * J, span_s * J), BF16),
            pltpu.VMEM((2, G * cols, G * span_r), BF16),
            pltpu.VMEM((2, LAYERS, 3 * lanes, lanes), BF16),
            pltpu.VMEM((jw, nodes), BF16),
            pltpu.VMEM((nodes, jw), BF16),
            pltpu.VMEM((n_sta, 8, lanes), F32),
            pltpu.VMEM((w_rows, lanes), F32),
            pltpu.VMEM((n_sta, chunk, lanes), F32),
            pltpu.VMEM((n_src, chunk, lanes), F32),
            pltpu.VMEM((w_rows, lanes), F32),
            dma((2 * LAYERS, 4)),
            dma((2 * LAYERS, 4)),
            dma((n_sta,)),
            dma((n_sta,)),
            dma((n_sta,)),
            dma((n_sta,)),
            dma((n_src,)),
            dma((n_src,)),
            dma((n_sta,)),
            dma((n_sta,)),
        ],
        compiler_params=pltpu.CompilerParams(
            collective_id=0, has_side_effects=True, vmem_limit_bytes=48 * 1024 * 1024
        ),
    )(
        features,
        station_lists,
        station_counts.reshape(1, -1),
        source_lists,
        source_counts.reshape(1, -1),
        picks,
        targets,
        layer_weights,
        readout_vector.reshape(1, -1),
    )
    node_total = jnp.float32(rows * n_sta) * jnp.float32(cols * n_src)
    factor = 1.0 / jnp.sqrt(node_total)
    blocks = w_sum[: 3 * feature].reshape(3, feature, 2, feature).transpose(0, 2, 3, 1)
    w_total = jnp.stack(
        [jnp.concatenate([blocks[l], blocks[2, l : l + 1]], 0) for l in range(LAYERS)]
    )
    v_total = jnp.sum(w_sum[3 * feature].reshape(windows, feature), axis=0)
    return (lik, grad, w_total * factor, v_total * factor)


def solution(mesh):
    in_specs = (P("sta", "src", None), P(), P(), P(), P(), P(None, "sta"), P(None, "src"), P(), P())
    out_specs = (P(None, "src"), P("sta", "src", None), P(), P())
    body = functools.partial(shards, mesh.shape["sta"], mesh.shape["src"])
    return jax.shard_map(body, mesh=mesh, in_specs=in_specs, out_specs=out_specs, check_vma=False)
```

time: 296 us -> 56.5 us (0.19)
  waiting for transfers between devices: 135 us -> 0 us
  blocking collectives: 51.4 us -> 0 us
  Pallas kernels: 0 us -> 49.9 us
  starting transfers between devices: 39.2 us -> 0 us
  local copies, waits for them, and re-layouts: 31.2 us -> 4.13 us
  matrix products: 14.9 us -> 0 us
  between operations: 14.9 us -> 0.75 us
  other arithmetic: 7.36 us -> 1.26 us
    psum x1 -> x0, waiting for transfers between devices: 116 us -> none  [shards(): w_total, v_total = lax.psum((w_sum, v_sum), ('sta', 'src'))]
    psum x2 -> x0, blocking collectives: 51.4 us -> none  [the longest x1 42.1 us: shards(): w_total, v_total = lax.psum((w_sum, v_sum), ('sta', 'src'))]
    pallas_call x0 -> x1, Pallas kernels: none -> 49.9 us  [shards(): pl.pallas_call(functools.partial(kernel, n_sta, n_src, chunk), out_shape=...]
    ppermute x16 -> x0, starting transfers between devices: 39.1 us -> none  [the longest x8 28.6 us: padded_2(): lax.ppermute(tail, axis, [(i, (i + 1) % count) for i in range(ends)])]
    ppermute x16 -> x0, waiting for transfers between devices: 19.4 us -> none  [the longest x8 16.9 us: padded_2(): lax.ppermute(head, axis, [((i + 1) % count, i) for i in range(ends)])]
    dot_general x24 -> x0, matrix products: 14.9 us -> none  [the longest x8 5.09 us: apply_block(): jnp.dot(flat, matrix, preferred_element_type=jnp.float32)]
    unnamed x95 -> x20, local copies, waits for them, and re-layouts: 12.8 us -> 3.73 us
    reshape x9 -> x2, local copies, waits for them, and re-layouts: 7.91 us -> 0.27 us  [shards(): w_sum[:3 * feature].reshape(3, feature, 2, feature).transpose(0, 2, 3, 1)]
  transfers between devices with their start and end apart: 17 -> 0, of which waited for: 7 -> 0; matrix products, arithmetic and copies ran while one was open for 5% -> 0% of each run, Pallas kernels for 0% -> 0%
where the time goes in v1:
time: 56.5 us; the launch traced here: 56.1 us
  Pallas kernels  49.9 us (88%)
  local copies, waits for them, and re-layouts  4.13 us (7%)
  other arithmetic  1.26 us (2%)
  between operations  0.75 us (1%)
    pallas_call x1, Pallas kernels, shards(): pl.pallas_call(functools.partial(kernel, n_sta, n_src, chunk), out_shape=...  49.9 us
    unnamed x20, local copies, waits for them, and re-layouts  3.73 us
    mul x2, other arithmetic, shards(): return (lik, grad, w_total * factor, v_total * factor)  1.22 us

profile of v1, /device:TPU:0, one launch (start us, length us, event | category | flops | bytes accessed | tf_op | source)
XLA Modules:
  0.0 56.1 jit_solution(3106825697148155569)
XLA Ops:
  0.6 0.0 copy-start.7
  0.6 0.0 copy-start.1
  0.7 0.8 %copy.13.slist = s32[128,16]{1,0:T(8,128)S(1)} copy(s32[128,16]{0,1:T(8,128)} %param.10) | data formatting | bytes 16384 | tf_op args[1]
  1.5 0.0 copy-done.7
  1.5 0.0 copy-start.2
  1.5 0.0 copy-start.3
  1.5 0.0 copy-start.4
  1.5 0.0 copy-start.5
  1.5 0.0 copy-start.6
  1.5 0.1 copy.14.rlist
  1.6 0.0 copy-done.1
  1.7 0.5 copy-done.2
  2.2 0.0 copy-done.3
  2.2 0.0 copy-done.4
  2.2 0.0 copy-done.5
  2.2 0.0 copy-done.6
  2.2 0.0 copy-start
  2.2 0.9 %copy-done = bf16[32,32,128]{2,1,0:T(8,128)(2,1)S(1)} copy-done((bf16[32,32,128]{2,1,0:T(8,128)(2,1)S(1)}, bf16[32,32,128]{2,1,0:T(8,128)(2,1)}, u32[]{:S(2)}) %copy-start) | copy-done | bytes 262168
  3.2 49.9 %shard_map.120 = (f32[2,32]{1,0:T(2,128)S(1)}, bf16[32,32,128]{2,1,0:T(8,128)(2,1)S(1)}, f32[224,128]{1,0:T(8,128)S(1)}) custom-call(bf16[32,32,128]{2,1,0:T(8,128)(2,1)S(1)} %copy-done, s32[128,16]{1,0:T(8,128)S(1)} %copy.13.slist, s32[1,128]{1,0:T(1,128)S(1)} %bitcast.17, s32[256,16]{1,0:T(8,128)S(1)} %copy.14.rlist, s32[1,256]{1,0:T(1,128)S(1)} %bitcast.16, ...), custom_call_target="tpu_custom_call" | custom-call | tf_op jit(solution)/shard_map/pallas_call | solution.py:431
  53.1 0.1 reshape_squeeze.3
  53.2 0.5 broadcast_multiply_fusion
  53.8 0.2 reshape.23
  53.9 0.1 copy.15
  54.1 0.7 %maximum_multiply_fusion = f32[2,3,64,64]{3,2,1,0:T(8,128)} fusion(f32[1,3,64,64]{3,2,1,0:T(8,128)S(1)} %get-tuple-element.15, f32[1,3,64,64]{3,2,1,0:T(8,128)S(1)} %get-tuple-element.14), kind=kLoop, calls=%fused_computation | loop fusion | flops 49152 | bytes 196608 | tf_op jit(solution)/shard_map/mul | solution.py:488
  54.8 0.6 %copy.18 = f32[2,32]{1,0:T(2,128)} copy(f32[2,32]{1,0:T(2,128)S(1)} %get-tuple-element.20) | data formatting | bytes 512
  55.4 0.7 %copy.19 = bf16[32,32,128]{2,1,0:T(8,128)(2,1)} copy(bf16[32,32,128]{2,1,0:T(8,128)(2,1)S(1)} %get-tuple-element.21) | data formatting | bytes 524288
  (6 shorter events, 0.1 us)
Async XLA Ops:
  0.6 0.9 %copy-start.7 = (s32[256,16]{0,1:T(8,128)S(1)}, s32[256,16]{0,1:T(8,128)}, u32[]{:S(2)}) copy-start(s32[256,16]{0,1:T(8,128)} %param.12) | copy-start | bytes 49156
  0.6 1.0 %copy-start.1 = (bf16[2,3,64,64]{3,2,1,0:T(8,128)(2,1)S(1)}, bf16[2,3,64,64]{3,2,1,0:T(8,128)(2,1)}, u32[]{:S(2)}) copy-start(bf16[2,3,64,64]{3,2,1,0:T(8,128)(2,1)} %weights.1) | copy-start | bytes 147460
  1.5 0.7 %copy-start.2 = (s32[256]{0:T(256)S(1)}, s32[256]{0:T(256)}, u32[]{:S(2)}) copy-start(s32[256]{0:T(256)} %param.13) | copy-start | bytes 3076
  1.5 0.7 %copy-start.3 = (s32[2,32]{1,0:T(2,128)S(1)}, s32[2,32]{1,0:T(2,128)}, u32[]{:S(2)}) copy-start(s32[2,32]{1,0:T(2,128)} %picks.1) | copy-start | bytes 772
  1.5 0.7 %copy-start.4 = (f32[2,32]{1,0:T(2,128)S(1)}, f32[2,32]{1,0:T(2,128)}, u32[]{:S(2)}) copy-start(f32[2,32]{1,0:T(2,128)} %targets.1) | copy-start | bytes 772
  1.5 0.7 %copy-start.5 = (s32[128]{0:T(128)S(1)}, s32[128]{0:T(128)}, u32[]{:S(2)}) copy-start(s32[128]{0:T(128)} %param.11) | copy-start | bytes 1540
  1.5 0.7 %copy-start.6 = (bf16[64]{0:T(256)(128)(2,1)S(1)}, bf16[64]{0:T(256)(128)(2,1)}, u32[]{:S(2)}) copy-start(bf16[64]{0:T(256)(128)(2,1)} %param.17) | copy-start | bytes 388
  2.2 1.0 %copy-start = (bf16[32,32,128]{2,1,0:T(8,128)(2,1)S(1)}, bf16[32,32,128]{2,1,0:T(8,128)(2,1)}, u32[]{:S(2)}) copy-start(bf16[32,32,128]{2,1,0:T(8,128)(2,1)} %feat.1) | copy-start | bytes 786436

commit v2 on v1

v2 whole, which is shorter than its diff:
```python
import functools

import jax
import jax.numpy as jnp
import numpy as np
from jax import lax
from jax.experimental import pallas as pl
from jax.experimental.pallas import tpu as pltpu
from jax.sharding import PartitionSpec as P

LAYERS = 2
HW = 16
J = 16
G = 4
HALVES = 2
MESH = pl.DeviceIdType.MESH
F32, BF16 = jnp.float32, jnp.bfloat16


def iota(shape, dim):
    return lax.broadcasted_iota(jnp.int32, shape, dim)


def ones_where(cond):
    return jnp.where(cond, 1.0, 0.0).astype(BF16)


def dot(a, b):
    return lax.dot_general(a, b, (((1,), (0,)), ((), ())), preferred_element_type=F32)


def dot_nt(a, b):
    return lax.dot_general(a, b, (((1,), (1,)), ((), ())), preferred_element_type=F32)


def dot_tn(a, b):
    return lax.dot_general(a, b, (((0,), (0,)), ((), ())), preferred_element_type=F32)


def coefs(lists, count_row, base, span):
    total_rows = lists.shape[1]
    count = jnp.broadcast_to(count_row, (span, total_rows))
    place = iota((span, total_rows), 0) + base
    total = jnp.zeros((span, total_rows), F32)
    for k in range(lists.shape[0]):
        hit = (place == lists[k : k + 1]) & (count > float(k))
        total = total + jnp.where(hit, 1.0, 0.0)
    return (total / count).astype(BF16)


def kernel(
    n_sta,
    n_src,
    chunk,
    feat,
    slist,
    scnt,
    rlist,
    rcnt,
    picks,
    targets,
    weights,
    readout,
    lik_out,
    grad_out,
    w_out,
    hs,
    hr,
    x,
    xb,
    slope,
    ks,
    bd,
    wf,
    q,
    qt,
    lik_slots,
    w_local,
    sta_slots,
    src_slots,
    total,
    load_sem,
    halo_send,
    halo_recv,
    lik_send,
    lik_recv,
    a_send,
    a_recv,
    b_send,
    b_recv,
    c_send,
    c_recv,
):
    me_sta = lax.axis_index("sta")
    me_src = lax.axis_index("src")
    rows, cols, lanes = feat.shape
    feature = weights.shape[-1]
    windows = lanes // feature
    half = rows // HALVES
    span_s, span_r, span_h = rows + 2 * HW, cols + 2 * HW, half + 2 * HW
    nodes, part_nodes = rows * cols, half * cols
    all_sta, all_src = rows * n_sta, cols * n_src
    sta_first, src_first = me_sta * rows, me_src * cols

    def sta_peer(d):
        return lax.rem(me_sta + d, n_sta)

    def src_peer(d):
        return lax.rem(me_src + d, n_src)

    loads = [
        pltpu.make_async_copy(feat, hs.at[0, HW : HW + rows], load_sem.at[0]),
        pltpu.make_async_copy(feat, hr.at[0, :, HW : HW + cols], load_sem.at[1]),
        pltpu.make_async_copy(feat, x.at[0, :, :, 0:lanes], load_sem.at[2]),
    ]
    for copy in loads:
        copy.start()

    for e in range(2 * LAYERS):
        zero_s = jnp.zeros((HW, cols, lanes), BF16)
        zero_r = jnp.zeros((rows, HW, lanes), BF16)

        @pl.when(me_sta == 0)
        def _():
            hs[e, 0:HW] = zero_s

        @pl.when(me_sta == n_sta - 1)
        def _():
            hs[e, HW + rows :] = zero_s

        @pl.when(me_src == 0)
        def _():
            hr[e, :, 0:HW] = zero_r

        @pl.when(me_src == n_src - 1)
        def _():
            hr[e, :, HW + cols :] = zero_r

    barrier = pltpu.get_barrier_semaphore()
    for d in range(1, n_sta):
        pl.semaphore_signal(barrier, inc=1, device_id={"sta": sta_peer(d)}, device_id_type=MESH)
    for d in range(1, n_src):
        pl.semaphore_signal(barrier, inc=1, device_id={"src": src_peer(d)}, device_id_type=MESH)
    pl.semaphore_wait(barrier, n_sta + n_src - 2)

    def halo_copy(e, direction):
        h = (direction - 2) // 2
        own = slice(h * half, (h + 1) * half)
        if direction == 0:
            dst, device = hs.at[e, HW + rows :], {"sta": me_sta - 1}
            src = feat.at[0:HW] if e == 0 else hs.at[e, HW : 2 * HW]
        elif direction == 1:
            dst, device = hs.at[e, 0:HW], {"sta": me_sta + 1}
            src = feat.at[rows - HW :] if e == 0 else hs.at[e, rows : HW + rows]
        elif direction % 2 == 0:
            dst, device = hr.at[e, own, HW + cols :], {"src": me_src - 1}
            src = feat.at[own, 0:HW] if e == 0 else hr.at[e, own, HW : 2 * HW]
        else:
            dst, device = hr.at[e, own, 0:HW], {"src": me_src + 1}
            src = feat.at[own, cols - HW :] if e == 0 else hr.at[e, own, cols : HW + cols]
        return pltpu.make_async_remote_copy(
            src_ref=src,
            dst_ref=dst,
            send_sem=halo_send.at[e, direction],
            recv_sem=halo_recv.at[e, direction],
            device_id=device,
            device_id_type=MESH,
        )

    sides = [me_sta > 0, me_sta < n_sta - 1, me_src > 0, me_src < n_src - 1]

    def goes(direction):
        return sides[direction if direction < 2 else 2 + direction % 2]

    def comes(direction):
        return sides[1 - direction if direction < 2 else 3 - direction % 2]

    def halo_start(e, directions):
        for direction in directions:
            pl.when(goes(direction))(lambda: halo_copy(e, direction).start())

    def halo_wait(e, directions):
        for direction in directions:
            pl.when(comes(direction))(lambda: halo_copy(e, direction).wait_recv())

    def halo_drain(e):
        for direction in range(2 + 2 * HALVES):
            pl.when(goes(direction))(lambda: halo_copy(e, direction).wait_send())

    def halo_put(e, h, values):
        own = slice(h * half, (h + 1) * half)
        hr[e, own, HW : HW + cols] = values
        halo_start(e, (2 + 2 * h, 3 + 2 * h))
        hs[e, HW + h * half : HW + (h + 1) * half] = values
        halo_start(e, (h,))

    for h in range(HALVES):
        halo_start(0, (2 + 2 * h, 3 + 2 * h))
    halo_start(0, (0, 1))

    s_row, r_row = scnt[...].astype(F32), rcnt[...].astype(F32)
    s_lists, r_lists = slist[...], rlist[...]
    same_col = (iota((half * J, span_h * J), 0) % J) == (iota((half * J, span_h * J), 1) % J)
    same_grp = (iota((G * cols, G * span_r), 0) // cols) == (iota((G * cols, G * span_r), 1) // span_r)

    def put_mixes(way, left_s, cols_s, left_r, cols_r):
        left_s, left_r = left_s.astype(BF16), left_r.astype(BF16)
        for h in range(HALVES):
            right = cols_s[:, h * half * J : (h * half + span_h) * J]
            wide = dot(left_s[h * half * J : (h + 1) * half * J], right)
            ks[way, h] = jnp.where(same_col, wide, 0.0).astype(BF16)
        bd[way] = jnp.where(same_grp, dot(left_r, cols_r), 0.0).astype(BF16)

    def forward_mixes():
        fwd_s = coefs(s_lists, s_row, sta_first - HW, span_s)
        fwd_r = coefs(r_lists, r_row, src_first - HW, span_r)
        row_s = (rows * J, all_sta)
        row_r = (G * cols, all_src)
        put_mixes(
            0,
            dot_nt(ones_where(iota(row_s, 0) // J + sta_first == iota(row_s, 1)), fwd_s),
            ones_where((iota((span_s, span_s * J), 1) // J) == iota((span_s, span_s * J), 0)),
            dot_nt(ones_where(iota(row_r, 0) % cols + src_first == iota(row_r, 1)), fwd_r),
            ones_where((iota((span_r, G * span_r), 1) % span_r) == iota((span_r, G * span_r), 0)),
        )

    def backward_mixes():
        bwd_s = coefs(s_lists, s_row, sta_first, rows)
        bwd_r = coefs(r_lists, r_row, src_first, cols)
        col_s = (all_sta, span_s * J)
        col_r = (all_src, G * span_r)
        put_mixes(
            1,
            dot(ones_where((iota((rows * J, rows), 0) // J) == iota((rows * J, rows), 1)), bwd_s),
            ones_where(iota(col_s, 1) // J + (sta_first - HW) == iota(col_s, 0)),
            dot(ones_where((iota((G * cols, cols), 0) % cols) == iota((G * cols, cols), 1)), bwd_r),
            ones_where(iota(col_r, 1) % span_r + (src_first - HW) == iota(col_r, 0)),
        )

    spread = ones_where((iota((lanes, feature), 0) % feature) == iota((lanes, feature), 1))
    first_window = iota((feature, lanes), 1) < feature

    def put_weights():
        count = LAYERS * 3
        stack = weights[...].reshape(count * feature, feature)
        wide = dot_nt(stack, spread)
        double = jnp.concatenate([weights[n // 3, n % 3] for n in range(count) for _ in range(2)], axis=0)
        eye = ones_where(iota((feature, feature), 0) == iota((feature, feature), 1))
        turned = dot_nt(eye, double)
        for n in range(count):
            l, p = n // 3, n % 3
            for way, m in (
                (0, wide[n * feature : (n + 1) * feature]),
                (1, turned[:, n * lanes : (n + 1) * lanes]),
            ):
                top = slice(p * lanes, p * lanes + feature)
                low = slice(p * lanes + feature, (p + 1) * lanes)
                wf[way, l, top] = jnp.where(first_window, m, 0.0).astype(BF16)
                wf[way, l, low] = jnp.where(first_window, 0.0, m).astype(BF16)

    forward_mixes()
    put_weights()
    for copy in loads:
        copy.wait()

    def mix_sta(way, e, h, out):
        own = slice(h * half, (h + 1) * half)
        for j in range(0, cols, J):
            part = hs[e, h * half : h * half + span_h, j : j + J, :].reshape(span_h * J, lanes)
            mixed = dot(ks[way, h], part).astype(BF16)
            out[own, j : j + J, lanes : 2 * lanes] = mixed.reshape(half, J, lanes)

    def mix_src(way, e, h, out):
        for g in range(h * half, (h + 1) * half, G):
            part = hr[e, g : g + G].reshape(G * span_r, lanes)
            mixed = dot(bd[way], part).astype(BF16)
            out[g : g + G, :, 2 * lanes :] = mixed.reshape(G, cols, lanes)

    wide_readout = dot_nt(readout[...], spread)
    jw = windows * cols
    node_own = iota((jw, lanes), 0)
    win_mask = (node_own // cols) == (iota((jw, lanes), 1) // feature)
    diag = (node_own % cols) == iota((jw, lanes), 1)

    def to_column(row_of):
        wide = jnp.concatenate(
            [jnp.broadcast_to(row_of(w), (cols, lanes)) for w in range(windows)], axis=0
        )
        return jnp.sum(jnp.where(diag, wide, 0.0), axis=1, keepdims=True)

    picked = picks[...].astype(F32)
    for l in range(LAYERS):
        if l == 1:
            backward_mixes()
            wide_picks = jnp.concatenate(
                [jnp.broadcast_to(picked[w : w + 1], (cols, rows)) for w in range(windows)], axis=0
            ).astype(BF16)
            sel = ones_where((iota((nodes, rows), 0) // cols) == iota((nodes, rows), 1))
            at_q = (iota((jw, nodes), 0) % cols) == (iota((jw, nodes), 1) % cols)
            q[...] = jnp.where(at_q, dot_nt(wide_picks, sel), 0.0).astype(BF16)
            at_t = (iota((nodes, jw), 0) % cols) == (iota((nodes, jw), 1) % cols)
            qt[...] = jnp.where(at_t, dot_nt(sel, wide_picks), 0.0).astype(BF16)
        for h in range(HALVES):
            own = slice(h * half, (h + 1) * half)
            halo_wait(l, (1 - h,))
            mix_sta(0, l, h, x.at[l])
            halo_wait(l, (2 + 2 * h, 3 + 2 * h))
            mix_src(0, l, h, x.at[l])
            z = dot(x[l, own].reshape(part_nodes, 3 * lanes), wf[0, l])
            squashed = jnp.tanh(z)
            slope[l, h] = 1.0 - squashed * squashed
            before = x[l, own, :, 0:lanes].astype(F32)
            states = (before + squashed.reshape(half, cols, lanes)).astype(BF16)
            if l + 1 < LAYERS:
                halo_put(l + 1, h, states)
                x[l + 1, own, :, 0:lanes] = states
            else:
                xb[own, :, 0:lanes] = states

    heap = dot(q[...], xb[:, :, 0:lanes].reshape(nodes, lanes))
    score = jnp.sum(jnp.where(win_mask, heap * wide_readout, 0.0), axis=1, keepdims=True)
    flat = jnp.where(diag, score, 0.0)
    tile_row = iota((8, lanes), 0)
    tile = jnp.zeros((8, lanes), F32)
    for w in range(windows):
        part = jnp.sum(flat[w * cols : (w + 1) * cols], axis=0, keepdims=True)
        tile = jnp.where(tile_row == w, part, tile)
        count = jnp.sum(picked[w : w + 1], axis=1, keepdims=True)
        tile = jnp.where(tile_row == windows + w, count, tile)
    lik_slots[me_sta] = tile
    sends = []
    for d in range(1, n_sta):
        sends.append(
            pltpu.make_async_remote_copy(
                src_ref=lik_slots.at[me_sta],
                dst_ref=lik_slots.at[me_sta],
                send_sem=lik_send.at[d],
                recv_sem=lik_recv.at[d],
                device_id={"sta": sta_peer(d)},
                device_id_type=MESH,
            )
        )
        sends[-1].start()
    for copy in sends:
        copy.wait_recv()
    summed = lik_slots[0]
    for s in range(1, n_sta):
        summed = summed + lik_slots[s]
    root = jnp.sqrt(jnp.maximum(summed[windows : 2 * windows], 1.0))
    lik = summed[0:windows] / root
    lik_out[...] = lik[:, :cols]
    sig = jax.nn.sigmoid(lik)
    sig_col = to_column(lambda w: sig[w : w + 1])
    want = jnp.concatenate(
        [jnp.broadcast_to(targets[w : w + 1, :], (cols, cols)) for w in range(windows)], axis=0
    )
    diag_cols = (iota((jw, cols), 0) % cols) == iota((jw, cols), 1)
    want_col = jnp.sum(jnp.where(diag_cols, want, 0.0), axis=1, keepdims=True)
    err = (sig_col - want_col).astype(BF16).astype(F32)
    err_wide = jnp.where(win_mask, err, 0.0)
    v_row = jnp.sum(err_wide * heap, axis=0, keepdims=True)

    def put_delta(l, h, grad):
        delta = (grad * slope[l, h]).astype(BF16).reshape(half, cols, lanes)
        halo_put(2 * LAYERS - 1 - l, h, delta)
        xb[h * half : (h + 1) * half, :, 0:lanes] = delta

    grads = []
    for h in range(HALVES):
        spot = slice(h * part_nodes, (h + 1) * part_nodes)
        grads.append(dot(qt[spot], err_wide.astype(BF16)) * wide_readout)
        put_delta(LAYERS - 1, h, grads[h])

    def weight_sums(l):
        w_t = dot_tn(xb[:, :, 0:lanes].reshape(nodes, lanes), x[l].reshape(nodes, 3 * lanes))
        folded = []
        for p in range(3):
            both = jnp.where(
                first_window,
                w_t[0:feature, p * lanes : (p + 1) * lanes],
                w_t[feature:, p * lanes : (p + 1) * lanes],
            )
            folded.append(both + pltpu.roll(both, feature, 1))
        base = l * feature
        w_local[base : base + feature] = jnp.where(first_window, folded[0], folded[1])
        return folded[2]

    def chunk_of(ref, s):
        return ref.at[pl.ds(pl.multiple_of(s * chunk, 8), chunk)]

    first, second, third = [], [], []
    for l in reversed(range(LAYERS)):
        e = 2 * LAYERS - 1 - l
        if l == 1:
            kept = weight_sums(l)
        else:
            w_local[2 * feature : 3 * feature] = jnp.where(first_window, weight_sums(l), kept)
            w_local[3 * feature :] = jnp.broadcast_to(v_row, (w_local.shape[0] - 3 * feature, lanes))
            for d in range(1, n_sta):
                first.append(
                    pltpu.make_async_remote_copy(
                        src_ref=chunk_of(w_local, sta_peer(d)),
                        dst_ref=sta_slots.at[me_sta],
                        send_sem=a_send.at[d],
                        recv_sem=a_recv.at[d],
                        device_id={"sta": sta_peer(d)},
                        device_id_type=MESH,
                    )
                )
                first[-1].start()
            sta_slots[me_sta] = chunk_of(w_local, me_sta)[...]
        for h in range(HALVES):
            own = slice(h * half, (h + 1) * half)
            halo_wait(e, (1 - h,))
            mix_sta(1, e, h, xb)
            if l == 0 and h == 0:
                for copy in first:
                    copy.wait_recv()
                some = sta_slots[0]
                for s in range(1, n_sta):
                    some = some + sta_slots[s]
                src_slots[me_src] = some
                for d in range(1, n_src):
                    second.append(
                        pltpu.make_async_remote_copy(
                            src_ref=src_slots.at[me_src],
                            dst_ref=src_slots.at[me_src],
                            send_sem=b_send.at[d],
                            recv_sem=b_recv.at[d],
                            device_id={"src": src_peer(d)},
                            device_id_type=MESH,
                        )
                    )
                    second[-1].start()
            halo_wait(e, (2 + 2 * h, 3 + 2 * h))
            mix_src(1, e, h, xb)
            grad = grads[h] + dot(xb[own].reshape(part_nodes, 3 * lanes), wf[1, l])
            if l > 0:
                grads[h] = grad
                put_delta(l - 1, h, grad)
            else:
                grad_out[own] = grad.reshape(half, cols, lanes).astype(BF16)

    for copy in second:
        copy.wait_recv()
    some = src_slots[0]
    for s in range(1, n_src):
        some = some + src_slots[s]
    chunk_of(total, me_sta)[...] = some
    for d in range(1, n_sta):
        third.append(
            pltpu.make_async_remote_copy(
                src_ref=chunk_of(total, me_sta),
                dst_ref=chunk_of(total, me_sta),
                send_sem=c_send.at[d],
                recv_sem=c_recv.at[d],
                device_id={"sta": sta_peer(d)},
                device_id_type=MESH,
            )
        )
        third[-1].start()
    for e in range(2 * LAYERS):
        halo_drain(e)
    for copy in sends + first + second:
        copy.wait_send()
    for copy in third:
        copy.wait_recv()
    w_out[...] = total[...]
    for copy in third:
        copy.wait_send()


def finish(factor, windows, lik, grad, w_sum, lik_out, grad_out, w_out, v_out):
    lik_out[...] = lik[...]
    grad_out[...] = grad[...]
    feature = w_out.shape[-1]
    for t in range(3):
        turned = jnp.transpose(w_sum[t * feature : (t + 1) * feature] * factor)
        for n in range(2):
            l, p = (t, n) if t < 2 else (n, 2)
            w_out[l, p] = turned[n * feature : (n + 1) * feature]
    row = w_sum[3 * feature : 3 * feature + 1] * factor
    v_out[...] = (row + pltpu.roll(row, feature, 1))[:, :feature]


def shards(
    n_sta,
    n_src,
    features,
    station_lists,
    station_counts,
    source_lists,
    source_counts,
    picks,
    targets,
    layer_weights,
    readout_vector,
):
    rows, cols, lanes = features.shape
    feature = layer_weights.shape[-1]
    windows = lanes // feature
    nodes = rows * cols
    half = rows // HALVES
    span_s, span_r = rows + 2 * HW, cols + 2 * HW
    chunk = -(-(3 * feature + 1) // (8 * n_sta)) * 8
    w_rows = chunk * n_sta
    jw = windows * cols
    dma = pltpu.SemaphoreType.DMA
    vmem = pl.BlockSpec(memory_space=pltpu.VMEM)
    lik, grad, w_sum = pl.pallas_call(
        functools.partial(kernel, n_sta, n_src, chunk),
        out_shape=(
            jax.ShapeDtypeStruct((windows, cols), F32),
            jax.ShapeDtypeStruct((rows, cols, lanes), BF16),
            jax.ShapeDtypeStruct((w_rows, lanes), F32),
        ),
        in_specs=[pl.BlockSpec(memory_space=pl.ANY)] + [vmem] * 8,
        out_specs=(vmem,) * 3,
        scratch_shapes=[
            pltpu.VMEM((2 * LAYERS, span_s, cols, lanes), BF16),
            pltpu.VMEM((2 * LAYERS, rows, span_r, lanes), BF16),
            pltpu.VMEM((LAYERS, rows, cols, 3 * lanes), BF16),
            pltpu.VMEM((rows, cols, 3 * lanes), BF16),
            pltpu.VMEM((LAYERS, HALVES, nodes // HALVES, lanes), F32),
            pltpu.VMEM((2, HALVES, half * J, (half + 2 * HW) * J), BF16),
            pltpu.VMEM((2, G * cols, G * span_r), BF16),
            pltpu.VMEM((2, LAYERS, 3 * lanes, lanes), BF16),
            pltpu.VMEM((jw, nodes), BF16),
            pltpu.VMEM((nodes, jw), BF16),
            pltpu.VMEM((n_sta, 8, lanes), F32),
            pltpu.VMEM((w_rows, lanes), F32),
            pltpu.VMEM((n_sta, chunk, lanes), F32),
            pltpu.VMEM((n_src, chunk, lanes), F32),
            pltpu.VMEM((w_rows, lanes), F32),
            dma((3,)),
            dma((2 * LAYERS, 2 + 2 * HALVES)),
            dma((2 * LAYERS, 2 + 2 * HALVES)),
            dma((n_sta,)),
            dma((n_sta,)),
            dma((n_sta,)),
            dma((n_sta,)),
            dma((n_src,)),
            dma((n_src,)),
            dma((n_sta,)),
            dma((n_sta,)),
        ],
        compiler_params=pltpu.CompilerParams(
            collective_id=0, has_side_effects=True, vmem_limit_bytes=48 * 1024 * 1024
        ),
    )(
        features,
        station_lists.T,
        station_counts.reshape(1, -1),
        source_lists.T,
        source_counts.reshape(1, -1),
        picks,
        targets,
        layer_weights,
        readout_vector.reshape(1, -1),
    )
    factor = float(1.0 / np.sqrt(np.float32(rows * n_sta * cols * n_src)))
    lik, grad, w_total, v_total = pl.pallas_call(
        functools.partial(finish, factor, windows),
        out_shape=(
            jax.ShapeDtypeStruct(lik.shape, F32),
            jax.ShapeDtypeStruct(grad.shape, BF16),
            jax.ShapeDtypeStruct(layer_weights.shape, F32),
            jax.ShapeDtypeStruct((1, feature), F32),
        ),
        in_specs=[vmem] * 3,
        out_specs=(vmem,) * 4,
    )(lik, grad, w_sum)
    return (lik, grad, w_total, v_total.reshape(feature))


def solution(mesh):
    in_specs = (P("sta", "src", None), P(), P(), P(), P(), P(None, "sta"), P(None, "src"), P(), P())
    out_specs = (P(None, "src"), P("sta", "src", None), P(), P())
    body = functools.partial(shards, mesh.shape["sta"], mesh.shape["src"])
    return jax.shard_map(body, mesh=mesh, in_specs=in_specs, out_specs=out_specs, check_vma=False)
```

time: 56.5 us -> 55.7 us (0.986)
  local copies, waits for them, and re-layouts: 4.13 us -> 7.82 us
  Pallas kernels: 49.9 us -> 46.8 us
  other arithmetic: 1.26 us -> 0 us
    pallas_call x1, Pallas kernels: 49.9 us -> 45 us  [shards(): pl.pallas_call(functools.partial(kernel, n_sta, n_src, chunk), out_shape=...]
    unnamed x20 -> x24, local copies, waits for them, and re-layouts: 3.73 us -> 7.82 us
    pallas_call x0 -> x1, Pallas kernels: none -> 1.8 us  [shards(): pl.pallas_call(functools.partial(finish, factor, windows), out_shape=(jax...]
    mul x2 -> x0, other arithmetic: 1.22 us -> none  [shards(): return (lik, grad, w_total * factor, v_total * factor)]
where the time goes in v2:
time: 55.7 us; the launch traced here: 55.3 us
  Pallas kernels  46.8 us (84%)
  local copies, waits for them, and re-layouts  7.82 us (14%)
  between operations  0.68 us (1%)
    pallas_call x1, Pallas kernels, shards(): pl.pallas_call(functools.partial(kernel, n_sta, n_src, chunk), out_shape=...  45 us
    unnamed x24, local copies, waits for them, and re-layouts  7.82 us
    pallas_call x1, Pallas kernels, shards(): pl.pallas_call(functools.partial(finish, factor, windows), out_shape=(jax...  1.8 us

profile of v2, /device:TPU:0, one launch (start us, length us, event | category | flops | bytes accessed | tf_op | source)
XLA Modules:
  0.0 55.3 jit_solution(18308359313717992601)
XLA Ops:
  0.6 0.0 copy-start.5
  0.6 0.0 copy-start.6
  0.7 0.7 %copy-done.5 = s32[128,16]{0,1:T(8,128)S(1)} copy-done((s32[128,16]{0,1:T(8,128)S(1)}, s32[128,16]{0,1:T(8,128)}, u32[]{:S(2)}) %copy-start.5) | copy-done | bytes 8216
  1.3 0.0 copy-done.6
  1.3 0.0 copy-start
  1.3 0.9 %copy-done = bf16[32,32,128]{2,1,0:T(8,128)(2,1)S(1)} copy-done((bf16[32,32,128]{2,1,0:T(8,128)(2,1)S(1)}, bf16[32,32,128]{2,1,0:T(8,128)(2,1)}, u32[]{:S(2)}) %copy-start) | copy-done | bytes 262168
  2.3 0.0 copy-start.3
  2.3 0.9 %copy-done.3 = bf16[2,3,64,64]{3,2,1,0:T(8,128)(2,1)S(1)} copy-done((bf16[2,3,64,64]{3,2,1,0:T(8,128)(2,1)S(1)}, bf16[2,3,64,64]{3,2,1,0:T(8,128)(2,1)}, u32[]{:S(2)}) %copy-start.3) | copy-done | bytes 49176
  3.2 0.0 copy-start.4
  3.2 0.7 %copy-done.4 = s32[256,16]{0,1:T(8,128)S(1)} copy-done((s32[256,16]{0,1:T(8,128)S(1)}, s32[256,16]{0,1:T(8,128)}, u32[]{:S(2)}) %copy-start.4) | copy-done | bytes 16408
  3.9 0.0 copy-start.7
  3.9 0.7 %copy-done.7 = s32[2,32]{1,0:T(2,128)S(1)} copy-done((s32[2,32]{1,0:T(2,128)S(1)}, s32[2,32]{1,0:T(2,128)}, u32[]{:S(2)}) %copy-start.7) | copy-done | bytes 280
  4.6 0.0 copy-start.8
  4.6 0.7 %copy-done.8 = f32[2,32]{1,0:T(2,128)S(1)} copy-done((f32[2,32]{1,0:T(2,128)S(1)}, f32[2,32]{1,0:T(2,128)}, u32[]{:S(2)}) %copy-start.8) | copy-done | bytes 280
  5.3 0.0 copy-start.10
  5.3 0.7 %copy-done.10 = s32[128]{0:T(128)S(1)} copy-done((s32[128]{0:T(128)S(1)}, s32[128]{0:T(128)}, u32[]{:S(2)}) %copy-start.10) | copy-done | bytes 536
  5.9 0.0 copy-start.11
  5.9 0.7 %copy-done.11 = bf16[64]{0:T(256)(128)(2,1)S(1)} copy-done((bf16[64]{0:T(256)(128)(2,1)S(1)}, bf16[64]{0:T(256)(128)(2,1)}, u32[]{:S(2)}) %copy-start.11) | copy-done | bytes 152
  6.6 45.0 %shard_map.120 = (f32[2,32]{1,0:T(2,128)S(1)}, bf16[32,32,128]{2,1,0:T(8,128)(2,1)S(1)}, f32[224,128]{1,0:T(8,128)S(1)}) custom-call(bf16[32,32,128]{2,1,0:T(8,128)(2,1)S(1)} %copy-done, s32[16,128]{1,0:T(8,128)S(1)} %bitcast.7, s32[1,128]{1,0:T(1,128)S(1)} %bitcast.9, s32[16,256]{1,0:T(8,128)S(1)} %bitcast.6, s32[1,256]{1,0:T(1,128)S(1)} %bitcast.8, ...), custom_call_target="tpu_custom_call" | custom-call | tf_op jit(solution)/shard_map/pallas_call | solution.py:510
  51.6 0.0 copy-start.1
  51.6 0.7 %copy-done.1 = bf16[32,32,128]{2,1,0:T(8,128)(2,1)} copy-done((bf16[32,32,128]{2,1,0:T(8,128)(2,1)}, bf16[32,32,128]{2,1,0:T(8,128)(2,1)S(1)}, u32[]{:S(2)}) %copy-start.1) | copy-done | bytes 262168
  52.3 0.0 copy-start.2
  52.3 0.6 %copy-done.2 = f32[224,128]{1,0:T(8,128)} copy-done((f32[224,128]{1,0:T(8,128)}, f32[224,128]{1,0:T(8,128)S(1)}, u32[]{:S(2)}) %copy-start.2) | copy-done | bytes 114712
  53.0 0.0 copy-start.9
  53.0 0.6 %copy-done.9 = f32[2,32]{1,0:T(2,128)} copy-done((f32[2,32]{1,0:T(2,128)}, f32[2,32]{1,0:T(2,128)S(1)}, u32[]{:S(2)}) %copy-start.9) | copy-done | bytes 280
  53.5 1.8 %shard_map.121 = (f32[2,32]{1,0:T(2,128)}, bf16[32,32,128]{2,1,0:T(8,128)(2,1)}, f32[2,3,64,64]{3,2,1,0:T(8,128)}, f32[1,64]{1,0:T(1,128)}) custom-call(f32[2,32]{1,0:T(2,128)} %copy-done.9, bf16[32,32,128]{2,1,0:T(8,128)(2,1)} %copy-done.1, f32[224,128]{1,0:T(8,128)} %copy-done.2), custom_call_target="tpu_custom_call" | custom-call | tf_op jit(solution)/shard_map/pallas_call | solution.py:562
Async XLA Ops:
  0.6 0.7 %copy-start.5 = (s32[128,16]{0,1:T(8,128)S(1)}, s32[128,16]{0,1:T(8,128)}, u32[]{:S(2)}) copy-start(s32[128,16]{0,1:T(8,128)} %param.10) | copy-start | bytes 24580
  0.6 0.7 %copy-start.6 = (s32[256]{0:T(256)S(1)}, s32[256]{0:T(256)}, u32[]{:S(2)}) copy-start(s32[256]{0:T(256)} %param.13) | copy-start | bytes 3076
  1.3 1.0 %copy-start = (bf16[32,32,128]{2,1,0:T(8,128)(2,1)S(1)}, bf16[32,32,128]{2,1,0:T(8,128)(2,1)}, u32[]{:S(2)}) copy-start(bf16[32,32,128]{2,1,0:T(8,128)(2,1)} %feat.1) | copy-start | bytes 786436
  2.3 0.9 %copy-start.3 = (bf16[2,3,64,64]{3,2,1,0:T(8,128)(2,1)S(1)}, bf16[2,3,64,64]{3,2,1,0:T(8,128)(2,1)}, u32[]{:S(2)}) copy-start(bf16[2,3,64,64]{3,2,1,0:T(8,128)(2,1)} %weights.1) | copy-start | bytes 147460
  3.2 0.7 %copy-start.4 = (s32[256,16]{0,1:T(8,128)S(1)}, s32[256,16]{0,1:T(8,128)}, u32[]{:S(2)}) copy-start(s32[256,16]{0,1:T(8,128)} %param.12) | copy-start | bytes 49156
  3.9 0.7 %copy-start.7 = (s32[2,32]{1,0:T(2,128)S(1)}, s32[2,32]{1,0:T(2,128)}, u32[]{:S(2)}) copy-start(s32[2,32]{1,0:T(2,128)} %picks.1) | copy-start | bytes 772
  4.6 0.7 %copy-start.8 = (f32[2,32]{1,0:T(2,128)S(1)}, f32[2,32]{1,0:T(2,128)}, u32[]{:S(2)}) copy-start(f32[2,32]{1,0:T(2,128)} %targets.1) | copy-start | bytes 772
  5.3 0.7 %copy-start.10 = (s32[128]{0:T(128)S(1)}, s32[128]{0:T(128)}, u32[]{:S(2)}) copy-start(s32[128]{0:T(128)} %param.11) | copy-start | bytes 1540
  5.9 0.7 %copy-start.11 = (bf16[64]{0:T(256)(128)(2,1)S(1)}, bf16[64]{0:T(256)(128)(2,1)}, u32[]{:S(2)}) copy-start(bf16[64]{0:T(256)(128)(2,1)} %param.17) | copy-start | bytes 388
  51.6 0.7 %copy-start.1 = (bf16[32,32,128]{2,1,0:T(8,128)(2,1)}, bf16[32,32,128]{2,1,0:T(8,128)(2,1)S(1)}, u32[]{:S(2)}) copy-start(bf16[32,32,128]{2,1,0:T(8,128)(2,1)S(1)} %get-tuple-element.12.grad) | copy-start | bytes 786436
  52.3 0.6 %copy-start.2 = (f32[224,128]{1,0:T(8,128)}, f32[224,128]{1,0:T(8,128)S(1)}, u32[]{:S(2)}) copy-start(f32[224,128]{1,0:T(8,128)S(1)} %get-tuple-element.13.w_sum) | copy-start | bytes 344068
  53.0 0.6 %copy-start.9 = (f32[2,32]{1,0:T(2,128)}, f32[2,32]{1,0:T(2,128)S(1)}, u32[]{:S(2)}) copy-start(f32[2,32]{1,0:T(2,128)S(1)} %get-tuple-element.11.lik) | copy-start | bytes 772

commit v3 on v2

--- a/solution.py
+++ b/solution.py
@@ -13,6 +13,7 @@
 J = 16
 G = 4
 HALVES = 2
+VMEM = 60 * 1024 * 1024
 MESH = pl.DeviceIdType.MESH
 F32, BF16 = jnp.float32, jnp.bfloat16
 
@@ -23,6 +24,14 @@
 
 def ones_where(cond):
     return jnp.where(cond, 1.0, 0.0).astype(BF16)
+
+
+def over(value, size):
+    return lax.shift_right_logical(value, jnp.full(value.shape, size.bit_length() - 1, jnp.int32))
+
+
+def within(value, size):
+    return value & (size - 1)
 
 
 def dot(a, b):
@@ -45,7 +54,7 @@
     for k in range(lists.shape[0]):
         hit = (place == lists[k : k + 1]) & (count > float(k))
         total = total + jnp.where(hit, 1.0, 0.0)
-    return (total / count).astype(BF16)
+    return (total * (1.0 / count_row)).astype(BF16)
 
 
 def kernel(
@@ -53,6 +62,17 @@
     n_src,
     chunk,
     feat,
+    slist_hbm,
+    scnt_hbm,
+    rlist_hbm,
+    rcnt_hbm,
+    picks_hbm,
+    targets_hbm,
+    weights_hbm,
+    readout_hbm,
+    lik_hbm,
+    grad_hbm,
+    w_hbm,
     slist,
     scnt,
     rlist,
@@ -63,7 +83,6 @@
     readout,
     lik_out,
     grad_out,
-    w_out,
     hs,
     hr,
     x,
@@ -80,6 +99,7 @@
     src_slots,
     total,
     load_sem,
+    out_sem,
     halo_send,
     halo_recv,
     lik_send,
@@ -113,7 +133,18 @@
         pltpu.make_async_copy(feat, hr.at[0, :, HW : HW + cols], load_sem.at[1]),
         pltpu.make_async_copy(feat, x.at[0, :, :, 0:lanes], load_sem.at[2]),
     ]
-    for copy in loads:
+    pairs = [
+        (slist_hbm, slist),
+        (scnt_hbm, scnt),
+        (rlist_hbm, rlist),
+        (rcnt_hbm, rcnt),
+        (picks_hbm, picks),
+        (targets_hbm, targets),
+        (weights_hbm, weights),
+        (readout_hbm, readout),
+    ]
+    small = [pltpu.make_async_copy(a, b, load_sem.at[3 + n]) for n, (a, b) in enumerate(pairs)]
+    for copy in small + loads:
         copy.start()
 
     for e in range(2 * LAYERS):
@@ -141,6 +172,36 @@
         pl.semaphore_signal(barrier, inc=1, device_id={"sta": sta_peer(d)}, device_id_type=MESH)
     for d in range(1, n_src):
         pl.semaphore_signal(barrier, inc=1, device_id={"src": src_peer(d)}, device_id_type=MESH)
+
+    for copy in small:
+        copy.wait()
+    s_row, r_row = scnt[...].astype(F32), rcnt[...].astype(F32)
+    s_lists, r_lists = slist[...], rlist[...]
+    same_col = within(iota((half * J, span_h * J), 0), J) == within(iota((half * J, span_h * J), 1), J)
+    same_grp = over(iota((G * cols, G * span_r), 0), cols) == over(iota((G * cols, G * span_r), 1), span_r)
+
+    def put_mixes(way, left_s, cols_s, left_r, cols_r):
+        left_s, left_r = left_s.astype(BF16), left_r.astype(BF16)
+        for h in range(HALVES):
+            right = cols_s[:, h * half * J : (h * half + span_h) * J]
+            wide = dot(left_s[h * half * J : (h + 1) * half * J], right)
+            ks[way, h] = jnp.where(same_col, wide, 0.0).astype(BF16)
+        bd[way] = jnp.where(same_grp, dot(left_r, cols_r), 0.0).astype(BF16)
+
+    def forward_mixes():
+        fwd_s = coefs(s_lists, s_row, sta_first - HW, span_s)
+        fwd_r = coefs(r_lists, r_row, src_first - HW, span_r)
+        row_s = (rows * J, all_sta)
+        row_r = (G * cols, all_src)
+        put_mixes(
+            0,
+            dot_nt(ones_where(over(iota(row_s, 0), J) + sta_first == iota(row_s, 1)), fwd_s),
+            ones_where(over(iota((span_s, span_s * J), 1), J) == iota((span_s, span_s * J), 0)),
+            dot_nt(ones_where(within(iota(row_r, 0), cols) + src_first == iota(row_r, 1)), fwd_r),
+            ones_where(within(iota((span_r, G * span_r), 1), span_r) == iota((span_r, G * span_r), 0)),
+        )
+
+    forward_mixes()
     pl.semaphore_wait(barrier, n_sta + n_src - 2)
 
     def halo_copy(e, direction):
@@ -198,32 +259,6 @@
         halo_start(0, (2 + 2 * h, 3 + 2 * h))
     halo_start(0, (0, 1))
 
-    s_row, r_row = scnt[...].astype(F32), rcnt[...].astype(F32)
-    s_lists, r_lists = slist[...], rlist[...]
-    same_col = (iota((half * J, span_h * J), 0) % J) == (iota((half * J, span_h * J), 1) % J)
-    same_grp = (iota((G * cols, G * span_r), 0) // cols) == (iota((G * cols, G * span_r), 1) // span_r)
-
-    def put_mixes(way, left_s, cols_s, left_r, cols_r):
-        left_s, left_r = left_s.astype(BF16), left_r.astype(BF16)
-        for h in range(HALVES):
-            right = cols_s[:, h * half * J : (h * half + span_h) * J]
-            wide = dot(left_s[h * half * J : (h + 1) * half * J], right)
-            ks[way, h] = jnp.where(same_col, wide, 0.0).astype(BF16)
-        bd[way] = jnp.where(same_grp, dot(left_r, cols_r), 0.0).astype(BF16)
-
-    def forward_mixes():
-        fwd_s = coefs(s_lists, s_row, sta_first - HW, span_s)
-        fwd_r = coefs(r_lists, r_row, src_first - HW, span_r)
-        row_s = (rows * J, all_sta)
-        row_r = (G * cols, all_src)
-        put_mixes(
-            0,
-            dot_nt(ones_where(iota(row_s, 0) // J + sta_first == iota(row_s, 1)), fwd_s),
-            ones_where((iota((span_s, span_s * J), 1) // J) == iota((span_s, span_s * J), 0)),
-            dot_nt(ones_where(iota(row_r, 0) % cols + src_first == iota(row_r, 1)), fwd_r),
-            ones_where((iota((span_r, G * span_r), 1) % span_r) == iota((span_r, G * span_r), 0)),
-        )
-
     def backward_mixes():
         bwd_s = coefs(s_lists, s_row, sta_first, rows)
         bwd_r = coefs(r_lists, r_row, src_first, cols)
@@ -231,13 +266,13 @@
         col_r = (all_src, G * span_r)
         put_mixes(
             1,
-            dot(ones_where((iota((rows * J, rows), 0) // J) == iota((rows * J, rows), 1)), bwd_s),
-            ones_where(iota(col_s, 1) // J + (sta_first - HW) == iota(col_s, 0)),
-            dot(ones_where((iota((G * cols, cols), 0) % cols) == iota((G * cols, cols), 1)), bwd_r),
-            ones_where(iota(col_r, 1) % span_r + (src_first - HW) == iota(col_r, 0)),
+            dot(ones_where(over(iota((rows * J, rows), 0), J) == iota((rows * J, rows), 1)), bwd_s),
+            ones_where(over(iota(col_s, 1), J) + (sta_first - HW) == iota(col_s, 0)),
+            dot(ones_where(within(iota((G * cols, cols), 0), cols) == iota((G * cols, cols), 1)), bwd_r),
+            ones_where(within(iota(col_r, 1), span_r) + (src_first - HW) == iota(col_r, 0)),
         )
 
-    spread = ones_where((iota((lanes, feature), 0) % feature) == iota((lanes, feature), 1))
+    spread = ones_where(within(iota((lanes, feature), 0), feature) == iota((lanes, feature), 1))
     first_window = iota((feature, lanes), 1) < feature
 
     def put_weights():
@@ -258,7 +293,6 @@
                 wf[way, l, top] = jnp.where(first_window, m, 0.0).astype(BF16)
                 wf[way, l, low] = jnp.where(first_window, 0.0, m).astype(BF16)
 
-    forward_mixes()
     put_weights()
     for copy in loads:
         copy.wait()
@@ -279,8 +313,8 @@
     wide_readout = dot_nt(readout[...], spread)
     jw = windows * cols
     node_own = iota((jw, lanes), 0)
-    win_mask = (node_own // cols) == (iota((jw, lanes), 1) // feature)
-    diag = (node_own % cols) == iota((jw, lanes), 1)
+    win_mask = over(node_own, cols) == over(iota((jw, lanes), 1), feature)
+    diag = within(node_own, cols) == iota((jw, lanes), 1)
 
     def to_column(row_of):
         wide = jnp.concatenate(
@@ -295,18 +329,19 @@
             wide_picks = jnp.concatenate(
                 [jnp.broadcast_to(picked[w : w + 1], (cols, rows)) for w in range(windows)], axis=0
             ).astype(BF16)
-            sel = ones_where((iota((nodes, rows), 0) // cols) == iota((nodes, rows), 1))
-            at_q = (iota((jw, nodes), 0) % cols) == (iota((jw, nodes), 1) % cols)
+            sel = ones_where(over(iota((nodes, rows), 0), cols) == iota((nodes, rows), 1))
+            at_q = within(iota((jw, nodes), 0), cols) == within(iota((jw, nodes), 1), cols)
             q[...] = jnp.where(at_q, dot_nt(wide_picks, sel), 0.0).astype(BF16)
-            at_t = (iota((nodes, jw), 0) % cols) == (iota((nodes, jw), 1) % cols)
+            at_t = within(iota((nodes, jw), 0), cols) == within(iota((nodes, jw), 1), cols)
             qt[...] = jnp.where(at_t, dot_nt(sel, wide_picks), 0.0).astype(BF16)
         for h in range(HALVES):
             own = slice(h * half, (h + 1) * half)
             halo_wait(l, (1 - h,))
             mix_sta(0, l, h, x.at[l])
+            z = dot(x[l, own, :, 0 : 2 * lanes].reshape(part_nodes, 2 * lanes), wf[0, l, 0 : 2 * lanes])
             halo_wait(l, (2 + 2 * h, 3 + 2 * h))
             mix_src(0, l, h, x.at[l])
-            z = dot(x[l, own].reshape(part_nodes, 3 * lanes), wf[0, l])
+            z = z + dot(x[l, own, :, 2 * lanes :].reshape(part_nodes, lanes), wf[0, l, 2 * lanes :])
             squashed = jnp.tanh(z)
             slope[l, h] = 1.0 - squashed * squashed
             before = x[l, own, :, 0:lanes].astype(F32)
@@ -349,12 +384,14 @@
     root = jnp.sqrt(jnp.maximum(summed[windows : 2 * windows], 1.0))
     lik = summed[0:windows] / root
     lik_out[...] = lik[:, :cols]
+    outs = [pltpu.make_async_copy(lik_out, lik_hbm, out_sem.at[HALVES])]
+    outs[0].start()
     sig = jax.nn.sigmoid(lik)
     sig_col = to_column(lambda w: sig[w : w + 1])
     want = jnp.concatenate(
         [jnp.broadcast_to(targets[w : w + 1, :], (cols, cols)) for w in range(windows)], axis=0
     )
-    diag_cols = (iota((jw, cols), 0) % cols) == iota((jw, cols), 1)
+    diag_cols = within(iota((jw, cols), 0), cols) == iota((jw, cols), 1)
     want_col = jnp.sum(jnp.where(diag_cols, want, 0.0), axis=1, keepdims=True)
     err = (sig_col - want_col).astype(BF16).astype(F32)
     err_wide = jnp.where(win_mask, err, 0.0)
@@ -432,14 +469,19 @@
                         )
                     )
                     second[-1].start()
+            early = xb[own, :, 0 : 2 * lanes].reshape(part_nodes, 2 * lanes)
+            grad = grads[h] + dot(early, wf[1, l, 0 : 2 * lanes])
             halo_wait(e, (2 + 2 * h, 3 + 2 * h))
             mix_src(1, e, h, xb)
-            grad = grads[h] + dot(xb[own].reshape(part_nodes, 3 * lanes), wf[1, l])
+            late = xb[own, :, 2 * lanes :].reshape(part_nodes, lanes)
+            grad = grad + dot(late, wf[1, l, 2 * lanes :])
             if l > 0:
                 grads[h] = grad
                 put_delta(l - 1, h, grad)
             else:
                 grad_out[own] = grad.reshape(half, cols, lanes).astype(BF16)
+                outs.append(pltpu.make_async_copy(grad_out.at[own], grad_hbm.at[own], out_sem.at[h]))
+                outs[-1].start()
 
     for copy in second:
         copy.wait_recv()
@@ -465,22 +507,32 @@
         copy.wait_send()
     for copy in third:
         copy.wait_recv()
-    w_out[...] = total[...]
+    outs.append(pltpu.make_async_copy(total, w_hbm, out_sem.at[HALVES + 1]))
+    outs[-1].start()
     for copy in third:
         copy.wait_send()
-
-
-def finish(factor, windows, lik, grad, w_sum, lik_out, grad_out, w_out, v_out):
-    lik_out[...] = lik[...]
-    grad_out[...] = grad[...]
+    for copy in outs:
+        copy.wait()
+
+
+def finish(factor, lik, grad, w_sum, lik_out, grad_out, w_out, v_out, sums, sems):
+    load = pltpu.make_async_copy(w_sum, sums, sems.at[0])
+    pass_grad = pltpu.make_async_copy(grad, grad_out, sems.at[1])
+    pass_lik = pltpu.make_async_copy(lik, lik_out, sems.at[2])
+    load.start()
+    pass_grad.start()
+    pass_lik.start()
+    load.wait()
     feature = w_out.shape[-1]
     for t in range(3):
-        turned = jnp.transpose(w_sum[t * feature : (t + 1) * feature] * factor)
+        turned = jnp.transpose(sums[t * feature : (t + 1) * feature] * factor)
         for n in range(2):
             l, p = (t, n) if t < 2 else (n, 2)
             w_out[l, p] = turned[n * feature : (n + 1) * feature]
-    row = w_sum[3 * feature : 3 * feature + 1] * factor
+    row = sums[3 * feature : 3 * feature + 1] * factor
     v_out[...] = (row + pltpu.roll(row, feature, 1))[:, :feature]
+    pass_grad.wait()
+    pass_lik.wait()
 
 
 def shards(
@@ -506,7 +558,19 @@
     w_rows = chunk * n_sta
     jw = windows * cols
     dma = pltpu.SemaphoreType.DMA
+    hbm = pl.BlockSpec(memory_space=pl.ANY)
     vmem = pl.BlockSpec(memory_space=pltpu.VMEM)
+    operands = (
+        features,
+        station_lists.T,
+        station_counts.reshape(1, -1),
+        source_lists.T,
+        source_counts.reshape(1, -1),
+        picks,
+        targets,
+        layer_weights,
+        readout_vector.reshape(1, -1),
+    )
     lik, grad, w_sum = pl.pallas_call(
         functools.partial(kernel, n_sta, n_src, chunk),
         out_shape=(
@@ -514,9 +578,12 @@
             jax.ShapeDtypeStruct((rows, cols, lanes), BF16),
             jax.ShapeDtypeStruct((w_rows, lanes), F32),
         ),
-        in_specs=[pl.BlockSpec(memory_space=pl.ANY)] + [vmem] * 8,
-        out_specs=(vmem,) * 3,
-        scratch_shapes=[
+        in_specs=[hbm] * 9,
+        out_specs=(hbm,) * 3,
+        scratch_shapes=[pltpu.VMEM(a.shape, a.dtype) for a in operands[1:]]
+        + [
+            pltpu.VMEM((windows, cols), F32),
+            pltpu.VMEM((rows, cols, lanes), BF16),
             pltpu.VMEM((2 * LAYERS, span_s, cols, lanes), BF16),
             pltpu.VMEM((2 * LAYERS, rows, span_r, lanes), BF16),
             pltpu.VMEM((LAYERS, rows, cols, 3 * lanes), BF16),
@@ -532,7 +599,8 @@
             pltpu.VMEM((n_sta, chunk, lanes), F32),
             pltpu.VMEM((n_src, chunk, lanes), F32),
             pltpu.VMEM((w_rows, lanes), F32),
-            dma((3,)),
+            dma((11,)),
+            dma((HALVES + 2,)),
             dma((2 * LAYERS, 2 + 2 * HALVES)),
             dma((2 * LAYERS, 2 + 2 * HALVES)),
             dma((n_sta,)),
@@ -545,30 +613,22 @@
             dma((n_sta,)),
         ],
         compiler_params=pltpu.CompilerParams(
-            collective_id=0, has_side_effects=True, vmem_limit_bytes=48 * 1024 * 1024
+            collective_id=0, has_side_effects=True, vmem_limit_bytes=VMEM
         ),
-    )(
-        features,
-        station_lists.T,
-        station_counts.reshape(1, -1),
-        source_lists.T,
-        source_counts.reshape(1, -1),
-        picks,
-        targets,
-        layer_weights,
-        readout_vector.reshape(1, -1),
-    )
+    )(*operands)
     factor = float(1.0 / np.sqrt(np.float32(rows * n_sta * cols * n_src)))
     lik, grad, w_total, v_total = pl.pallas_call(
-        functools.partial(finish, factor, windows),
+        functools.partial(finish, factor),
         out_shape=(
             jax.ShapeDtypeStruct(lik.shape, F32),
             jax.ShapeDtypeStruct(grad.shape, BF16),
             jax.ShapeDtypeStruct(layer_weights.shape, F32),
             jax.ShapeDtypeStruct((1, feature), F32),
         ),
-        in_specs=[vmem] * 3,
-        out_specs=(vmem,) * 4,
+        in_specs=[hbm] * 3,
+        out_specs=(hbm, hbm, vmem, vmem),
+        scratch_shapes=[pltpu.VMEM(w_sum.shape, F32), dma((3,))],
+        compiler_params=pltpu.CompilerParams(vmem_limit_bytes=VMEM),
     )(lik, grad, w_sum)
     return (lik, grad, w_total, v_total.reshape(feature))
 

time: 55.7 us -> 56.9 us (1.022)
  Pallas kernels: 46.8 us -> 56.1 us
  local copies, waits for them, and re-layouts: 7.82 us -> 0 us
    pallas_call x1, Pallas kernels: 1.8 us -> 9.78 us  [shards(): pl.pallas_call(functools.partial(finish, factor), out_shape=(jax.ShapeDty...]
    unnamed x24 -> x0, local copies, waits for them, and re-layouts: 7.82 us -> none
    pallas_call x1, Pallas kernels: 45 us -> 46.3 us  [shards(): pl.pallas_call(functools.partial(kernel, n_sta, n_src, chunk), out_shape=...]
where the time goes in v3:
time: 56.9 us; the launch traced here: 56.7 us
  Pallas kernels  56.1 us (99%)
  between operations  0.64 us (1%)
    pallas_call x1, Pallas kernels, shards(): pl.pallas_call(functools.partial(kernel, n_sta, n_src, chunk), out_shape=...  46.3 us
    pallas_call x1, Pallas kernels, shards(): pl.pallas_call(functools.partial(finish, factor), out_shape=(jax.ShapeDty...  9.78 us

profile of v3, /device:TPU:0, one launch (start us, length us, event | category | flops | bytes accessed | tf_op | source)
XLA Modules:
  0.0 56.7 jit_solution(2783759675151817997)
XLA Ops:
  0.6 46.3 %shard_map.120 = (f32[2,32]{1,0:T(2,128)}, bf16[32,32,128]{2,1,0:T(8,128)(2,1)}, f32[224,128]{1,0:T(8,128)}) custom-call(bf16[32,32,128]{2,1,0:T(8,128)(2,1)} %feat.1, s32[16,128]{1,0:T(8,128)} %bitcast.7, s32[1,128]{1,0:T(1,128)} %bitcast.9, s32[16,256]{1,0:T(8,128)} %bitcast.6, s32[1,256]{1,0:T(1,128)} %bitcast.8, s32[2,32]{1,0:T(2,128)} %picks_hbm.1, ...), custom_call_target="tpu_custom_call" | custom-call | tf_op jit(solution)/shard_map/pallas_call | solution.py:574
  46.9 9.8 %shard_map.121 = (f32[2,32]{1,0:T(2,128)}, bf16[32,32,128]{2,1,0:T(8,128)(2,1)}, f32[2,3,64,64]{3,2,1,0:T(8,128)}, f32[1,64]{1,0:T(1,128)}) custom-call(f32[2,32]{1,0:T(2,128)} %get-tuple-element.11.lik, bf16[32,32,128]{2,1,0:T(8,128)(2,1)} %get-tuple-element.12.grad, f32[224,128]{1,0:T(8,128)} %get-tuple-element.13.w_sum), custom_call_target="tpu_custom_call" | custom-call | tf_op jit(solution)/shard_map/pallas_call | solution.py:620

commit v4 on v3

--- a/solution.py
+++ b/solution.py
@@ -130,8 +130,6 @@
 
     loads = [
         pltpu.make_async_copy(feat, hs.at[0, HW : HW + rows], load_sem.at[0]),
-        pltpu.make_async_copy(feat, hr.at[0, :, HW : HW + cols], load_sem.at[1]),
-        pltpu.make_async_copy(feat, x.at[0, :, :, 0:lanes], load_sem.at[2]),
     ]
     pairs = [
         (slist_hbm, slist),
@@ -143,7 +141,7 @@
         (weights_hbm, weights),
         (readout_hbm, readout),
     ]
-    small = [pltpu.make_async_copy(a, b, load_sem.at[3 + n]) for n, (a, b) in enumerate(pairs)]
+    small = [pltpu.make_async_copy(a, b, load_sem.at[1 + n]) for n, (a, b) in enumerate(pairs)]
     for copy in small + loads:
         copy.start()
 
@@ -209,16 +207,16 @@
         own = slice(h * half, (h + 1) * half)
         if direction == 0:
             dst, device = hs.at[e, HW + rows :], {"sta": me_sta - 1}
-            src = feat.at[0:HW] if e == 0 else hs.at[e, HW : 2 * HW]
+            src = hs.at[e, HW : 2 * HW]
         elif direction == 1:
             dst, device = hs.at[e, 0:HW], {"sta": me_sta + 1}
-            src = feat.at[rows - HW :] if e == 0 else hs.at[e, rows : HW + rows]
+            src = hs.at[e, rows : HW + rows]
         elif direction % 2 == 0:
             dst, device = hr.at[e, own, HW + cols :], {"src": me_src - 1}
-            src = feat.at[own, 0:HW] if e == 0 else hr.at[e, own, HW : 2 * HW]
+            src = hr.at[e, own, HW : 2 * HW]
         else:
             dst, device = hr.at[e, own, 0:HW], {"src": me_src + 1}
-            src = feat.at[own, cols - HW :] if e == 0 else hr.at[e, own, cols : HW + cols]
+            src = hr.at[e, own, cols : HW + cols]
         return pltpu.make_async_remote_copy(
             src_ref=src,
             dst_ref=dst,
@@ -255,9 +253,14 @@
         hs[e, HW + h * half : HW + (h + 1) * half] = values
         halo_start(e, (h,))
 
+    for copy in loads:
+        copy.wait()
+    states = hs[0, HW : HW + rows]
+    hr[0, :, HW : HW + cols] = states
     for h in range(HALVES):
         halo_start(0, (2 + 2 * h, 3 + 2 * h))
     halo_start(0, (0, 1))
+    x[0, :, :, 0:lanes] = states
 
     def backward_mixes():
         bwd_s = coefs(s_lists, s_row, sta_first, rows)
@@ -294,8 +297,6 @@
                 wf[way, l, low] = jnp.where(first_window, 0.0, m).astype(BF16)
 
     put_weights()
-    for copy in loads:
-        copy.wait()
 
     def mix_sta(way, e, h, out):
         own = slice(h * half, (h + 1) * half)
@@ -423,7 +424,7 @@
         return folded[2]
 
     def chunk_of(ref, s):
-        return ref.at[pl.ds(pl.multiple_of(s * chunk, 8), chunk)]
+        return ref.at[pl.ds(pl.multiple_of(s * chunk, 16), chunk)]
 
     first, second, third = [], [], []
     for l in reversed(range(LAYERS)):
@@ -456,7 +457,7 @@
                 some = sta_slots[0]
                 for s in range(1, n_sta):
                     some = some + sta_slots[s]
-                src_slots[me_src] = some
+                src_slots[me_src] = some.astype(BF16)
                 for d in range(1, n_src):
                     second.append(
                         pltpu.make_async_remote_copy(
@@ -485,9 +486,9 @@
 
     for copy in second:
         copy.wait_recv()
-    some = src_slots[0]
+    some = src_slots[0].astype(F32)
     for s in range(1, n_src):
-        some = some + src_slots[s]
+        some = some + src_slots[s].astype(F32)
     chunk_of(total, me_sta)[...] = some
     for d in range(1, n_sta):
         third.append(
@@ -515,14 +516,22 @@
         copy.wait()
 
 
-def finish(factor, lik, grad, w_sum, lik_out, grad_out, w_out, v_out, sums, sems):
-    load = pltpu.make_async_copy(w_sum, sums, sems.at[0])
-    pass_grad = pltpu.make_async_copy(grad, grad_out, sems.at[1])
-    pass_lik = pltpu.make_async_copy(lik, lik_out, sems.at[2])
-    load.start()
-    pass_grad.start()
-    pass_lik.start()
-    load.wait()
+def finish(factor, lik, grad, w_sum, lik_out, grad_out, w_out, v_out, lik_buf, grad_buf, sums, sems):
+    loads = [
+        pltpu.make_async_copy(src, dst, sems.at[0, n])
+        for n, (src, dst) in enumerate(((grad, grad_buf), (w_sum, sums), (lik, lik_buf)))
+    ]
+    stores = [
+        pltpu.make_async_copy(src, dst, sems.at[1, n])
+        for n, (src, dst) in enumerate(((grad_buf, grad_out), (lik_buf, lik_out)))
+    ]
+    for copy in loads:
+        copy.start()
+    loads[0].wait()
+    stores[0].start()
+    loads[2].wait()
+    stores[1].start()
+    loads[1].wait()
     feature = w_out.shape[-1]
     for t in range(3):
         turned = jnp.transpose(sums[t * feature : (t + 1) * feature] * factor)
@@ -531,8 +540,8 @@
             w_out[l, p] = turned[n * feature : (n + 1) * feature]
     row = sums[3 * feature : 3 * feature + 1] * factor
     v_out[...] = (row + pltpu.roll(row, feature, 1))[:, :feature]
-    pass_grad.wait()
-    pass_lik.wait()
+    for copy in stores:
+        copy.wait()
 
 
 def shards(
@@ -554,7 +563,7 @@
     nodes = rows * cols
     half = rows // HALVES
     span_s, span_r = rows + 2 * HW, cols + 2 * HW
-    chunk = -(-(3 * feature + 1) // (8 * n_sta)) * 8
+    chunk = -(-(3 * feature + 1) // (16 * n_sta)) * 16
     w_rows = chunk * n_sta
     jw = windows * cols
     dma = pltpu.SemaphoreType.DMA
@@ -597,9 +606,9 @@
             pltpu.VMEM((n_sta, 8, lanes), F32),
             pltpu.VMEM((w_rows, lanes), F32),
             pltpu.VMEM((n_sta, chunk, lanes), F32),
-            pltpu.VMEM((n_src, chunk, lanes), F32),
+            pltpu.VMEM((n_src, chunk, lanes), BF16),
             pltpu.VMEM((w_rows, lanes), F32),
-            dma((11,)),
+            dma((9,)),
             dma((HALVES + 2,)),
             dma((2 * LAYERS, 2 + 2 * HALVES)),
             dma((2 * LAYERS, 2 + 2 * HALVES)),
@@ -627,7 +636,12 @@
         ),
         in_specs=[hbm] * 3,
         out_specs=(hbm, hbm, vmem, vmem),
-        scratch_shapes=[pltpu.VMEM(w_sum.shape, F32), dma((3,))],
+        scratch_shapes=[
+            pltpu.VMEM(lik.shape, F32),
+            pltpu.VMEM(grad.shape, BF16),
+            pltpu.VMEM(w_sum.shape, F32),
+            dma((2, 3)),
+        ],
         compiler_params=pltpu.CompilerParams(vmem_limit_bytes=VMEM),
     )(lik, grad, w_sum)
     return (lik, grad, w_total, v_total.reshape(feature))

time: 56.9 us -> 49.3 us (0.87)
  Pallas kernels: 56.1 us -> 48.5 us
    pallas_call x1, Pallas kernels: 9.78 us -> 2.39 us  [shards(): pl.pallas_call(functools.partial(finish, factor), out_shape=(jax.ShapeDty...]
where the time goes in v4:
time: 49.3 us; the launch traced here: 49.1 us
  Pallas kernels  48.5 us (98%)
  between operations  0.64 us (1%)
    pallas_call x1, Pallas kernels, shards(): pl.pallas_call(functools.partial(kernel, n_sta, n_src, chunk), out_shape=...  46.1 us
    pallas_call x1, Pallas kernels, shards(): pl.pallas_call(functools.partial(finish, factor), out_shape=(jax.ShapeDty...  2.39 us

profile of v4, /device:TPU:0, one launch (start us, length us, event | category | flops | bytes accessed | tf_op | source)
XLA Modules:
  0.0 49.1 jit_solution(12712279710513838942)
XLA Ops:
  0.6 46.1 %shard_map.120 = (f32[2,32]{1,0:T(2,128)}, bf16[32,32,128]{2,1,0:T(8,128)(2,1)}, f32[256,128]{1,0:T(8,128)}) custom-call(bf16[32,32,128]{2,1,0:T(8,128)(2,1)} %feat.1, s32[16,128]{1,0:T(8,128)} %bitcast.7, s32[1,128]{1,0:T(1,128)} %bitcast.9, s32[16,256]{1,0:T(8,128)} %bitcast.6, s32[1,256]{1,0:T(1,128)} %bitcast.8, s32[2,32]{1,0:T(2,128)} %picks_hbm.1, ...), custom_call_target="tpu_custom_call" | custom-call | tf_op jit(solution)/shard_map/pallas_call | solution.py:583
  46.7 2.4 %shard_map.121 = (f32[2,32]{1,0:T(2,128)}, bf16[32,32,128]{2,1,0:T(8,128)(2,1)}, f32[2,3,64,64]{3,2,1,0:T(8,128)}, f32[1,64]{1,0:T(1,128)}) custom-call(f32[2,32]{1,0:T(2,128)} %get-tuple-element.11.lik, bf16[32,32,128]{2,1,0:T(8,128)(2,1)} %get-tuple-element.12.grad, f32[256,128]{1,0:T(8,128)} %get-tuple-element.13.w_sum), custom_call_target="tpu_custom_call" | custom-call | tf_op jit(solution)/shard_map/pallas_call | solution.py:629

commit v5 on v4

--- a/solution.py
+++ b/solution.py
@@ -92,7 +92,6 @@
     bd,
     wf,
     q,
-    qt,
     lik_slots,
     w_local,
     sta_slots,
@@ -165,11 +164,34 @@
         def _():
             hr[e, :, HW + cols :] = zero_r
 
+    no_tiles = jnp.zeros((n_sta, 8, lanes), F32)
+
+    @pl.when(me_src == 0)
+    def _():
+        lik_slots[1] = no_tiles
+
+    @pl.when(me_src == n_src - 1)
+    def _():
+        lik_slots[2] = no_tiles
+
     barrier = pltpu.get_barrier_semaphore()
     for d in range(1, n_sta):
         pl.semaphore_signal(barrier, inc=1, device_id={"sta": sta_peer(d)}, device_id_type=MESH)
     for d in range(1, n_src):
         pl.semaphore_signal(barrier, inc=1, device_id={"src": src_peer(d)}, device_id_type=MESH)
+
+    beside = ((me_src > 0, -1), (me_src < n_src - 1, 1))
+    for near, step in beside:
+
+        @pl.when(near)
+        def _():
+            for d in range(1, n_sta):
+                pl.semaphore_signal(
+                    barrier,
+                    inc=1,
+                    device_id={"sta": sta_peer(d), "src": me_src + step},
+                    device_id_type=MESH,
+                )
 
     for copy in small:
         copy.wait()
@@ -200,7 +222,8 @@
         )
 
     forward_mixes()
-    pl.semaphore_wait(barrier, n_sta + n_src - 2)
+    blocks_beside = (me_src > 0).astype(jnp.int32) + (me_src < n_src - 1).astype(jnp.int32)
+    pl.semaphore_wait(barrier, n_sta + n_src - 2 + (n_sta - 1) * blocks_beside)
 
     def halo_copy(e, direction):
         h = (direction - 2) // 2
@@ -317,12 +340,6 @@
     win_mask = over(node_own, cols) == over(iota((jw, lanes), 1), feature)
     diag = within(node_own, cols) == iota((jw, lanes), 1)
 
-    def to_column(row_of):
-        wide = jnp.concatenate(
-            [jnp.broadcast_to(row_of(w), (cols, lanes)) for w in range(windows)], axis=0
-        )
-        return jnp.sum(jnp.where(diag, wide, 0.0), axis=1, keepdims=True)
-
     picked = picks[...].astype(F32)
     for l in range(LAYERS):
         if l == 1:
@@ -333,8 +350,6 @@
             sel = ones_where(over(iota((nodes, rows), 0), cols) == iota((nodes, rows), 1))
             at_q = within(iota((jw, nodes), 0), cols) == within(iota((jw, nodes), 1), cols)
             q[...] = jnp.where(at_q, dot_nt(wide_picks, sel), 0.0).astype(BF16)
-            at_t = within(iota((nodes, jw), 0), cols) == within(iota((nodes, jw), 1), cols)
-            qt[...] = jnp.where(at_t, dot_nt(sel, wide_picks), 0.0).astype(BF16)
         for h in range(HALVES):
             own = slice(h * half, (h + 1) * half)
             halo_wait(l, (1 - h,))
@@ -344,7 +359,10 @@
             mix_src(0, l, h, x.at[l])
             z = z + dot(x[l, own, :, 2 * lanes :].reshape(part_nodes, lanes), wf[0, l, 2 * lanes :])
             squashed = jnp.tanh(z)
-            slope[l, h] = 1.0 - squashed * squashed
+            slopes = 1.0 - squashed * squashed
+            slope[l, h] = slopes
+            if l == LAYERS - 1:
+                halo_put(LAYERS, h, slopes.astype(BF16).reshape(half, cols, lanes))
             before = x[l, own, :, 0:lanes].astype(F32)
             states = (before + squashed.reshape(half, cols, lanes)).astype(BF16)
             if l + 1 < LAYERS:
@@ -363,51 +381,94 @@
         tile = jnp.where(tile_row == w, part, tile)
         count = jnp.sum(picked[w : w + 1], axis=1, keepdims=True)
         tile = jnp.where(tile_row == windows + w, count, tile)
-    lik_slots[me_sta] = tile
-    sends = []
-    for d in range(1, n_sta):
-        sends.append(
-            pltpu.make_async_remote_copy(
-                src_ref=lik_slots.at[me_sta],
-                dst_ref=lik_slots.at[me_sta],
-                send_sem=lik_send.at[d],
-                recv_sem=lik_recv.at[d],
-                device_id={"sta": sta_peer(d)},
-                device_id_type=MESH,
-            )
+    lik_slots[0, me_sta] = tile
+    lik_slots[0, me_sta, 2 * windows : 3 * windows, 0:rows] = picked
+    lik_slots[0, me_sta, 3 * windows : 4 * windows, 0:cols] = targets[...]
+
+    def tile_copy(slot, d):
+        return pltpu.make_async_remote_copy(
+            src_ref=lik_slots.at[0, me_sta],
+            dst_ref=lik_slots.at[slot, me_sta],
+            send_sem=lik_send.at[slot, d],
+            recv_sem=lik_recv.at[slot, d],
+            device_id={"sta": sta_peer(d), "src": me_src + (0, 1, -1)[slot]},
+            device_id_type=MESH,
         )
-        sends[-1].start()
-    for copy in sends:
-        copy.wait_recv()
-    summed = lik_slots[0]
-    for s in range(1, n_sta):
-        summed = summed + lik_slots[s]
-    root = jnp.sqrt(jnp.maximum(summed[windows : 2 * windows], 1.0))
-    lik = summed[0:windows] / root
+
+    def tiles(act, coming):
+        for d in range(1, n_sta):
+            act(tile_copy(0, d))
+        for slot, side in ((1, 2 if coming else 3), (2, 3 if coming else 2)):
+
+            @pl.when(sides[side])
+            def _():
+                for d in range(n_sta):
+                    act(tile_copy(slot, d))
+
+    tiles(lambda copy: copy.start(), False)
+    halo_wait(LAYERS, range(2 + 2 * HALVES))
+    halo_drain(LAYERS)
+    tiles(lambda copy: copy.wait_recv(), True)
+
+    lane_window = over(iota((8, lanes), 1), feature)
+
+    def turn(values, row):
+        return dot_tn(values, jnp.where(tile_row == row + lane_window, 1.0, 0.0))
+
+    def error_of(slot):
+        summed = lik_slots[slot, 0]
+        for s in range(1, n_sta):
+            summed = summed + lik_slots[slot, s]
+        root = jnp.sqrt(jnp.maximum(summed[windows : 2 * windows], 1.0))
+        lik = summed[0:windows] / root
+        want = lik_slots[slot, 0, 3 * windows : 4 * windows]
+        err = (jax.nn.sigmoid(lik) - want).astype(BF16).astype(F32)
+        err = jnp.concatenate([err, jnp.zeros((8 - windows, lanes), F32)], axis=0)
+        return lik, turn(err, 0)[:cols]
+
+    lik, err_own = error_of(0)
     lik_out[...] = lik[:, :cols]
     outs = [pltpu.make_async_copy(lik_out, lik_hbm, out_sem.at[HALVES])]
     outs[0].start()
-    sig = jax.nn.sigmoid(lik)
-    sig_col = to_column(lambda w: sig[w : w + 1])
-    want = jnp.concatenate(
-        [jnp.broadcast_to(targets[w : w + 1, :], (cols, cols)) for w in range(windows)], axis=0
-    )
-    diag_cols = within(iota((jw, cols), 0), cols) == iota((jw, cols), 1)
-    want_col = jnp.sum(jnp.where(diag_cols, want, 0.0), axis=1, keepdims=True)
-    err = (sig_col - want_col).astype(BF16).astype(F32)
-    err_wide = jnp.where(win_mask, err, 0.0)
-    v_row = jnp.sum(err_wide * heap, axis=0, keepdims=True)
+    heap_own = jnp.where(win_mask, heap, 0.0)
+    heap_sum = heap_own[0:cols]
+    for w in range(1, windows):
+        heap_sum = heap_sum + heap_own[w * cols : (w + 1) * cols]
+    v_row = jnp.sum(err_own * heap_sum, axis=0, keepdims=True)
+    err_own = err_own * wide_readout
+    err_left = error_of(1)[1][cols - HW :] * wide_readout
+    err_right = error_of(2)[1][:HW] * wide_readout
+    picks_own = turn(lik_slots[0, me_sta], 2 * windows)
+    picks_up = turn(lik_slots[0, sta_peer(n_sta - 1)], 2 * windows)
+    picks_down = turn(lik_slots[0, sta_peer(1)], 2 * windows)
+
+    top = LAYERS
 
     def put_delta(l, h, grad):
         delta = (grad * slope[l, h]).astype(BF16).reshape(half, cols, lanes)
-        halo_put(2 * LAYERS - 1 - l, h, delta)
+        if l == LAYERS - 1:
+            hr[top, h * half : (h + 1) * half, HW : HW + cols] = delta
+            hs[top, HW + h * half : HW + (h + 1) * half] = delta
+        else:
+            halo_put(2 * LAYERS - 1 - l, h, delta)
         xb[h * half : (h + 1) * half, :, 0:lanes] = delta
+
+    def scaled(values, err, picked_row):
+        return (values.astype(F32) * (err * picked_row)).astype(BF16)
 
     grads = []
     for h in range(HALVES):
-        spot = slice(h * part_nodes, (h + 1) * part_nodes)
-        grads.append(dot(qt[spot], err_wide.astype(BF16)) * wide_readout)
+        spots = range(h * half, (h + 1) * half)
+        grads.append(jnp.concatenate([err_own * picks_own[i : i + 1] for i in spots], axis=0))
         put_delta(LAYERS - 1, h, grads[h])
+    for m in range(HW):
+        up = picks_up[rows - HW + m : rows - HW + m + 1]
+        hs[top, m] = scaled(hs[top, m], err_own, up)
+        hs[top, HW + rows + m] = scaled(hs[top, HW + rows + m], err_own, picks_down[m : m + 1])
+    for i in range(rows):
+        own_row = picks_own[i : i + 1]
+        hr[top, i, 0:HW] = scaled(hr[top, i, 0:HW], err_left, own_row)
+        hr[top, i, HW + cols :] = scaled(hr[top, i, HW + cols :], err_right, own_row)
 
     def weight_sums(l):
         w_t = dot_tn(xb[:, :, 0:lanes].reshape(nodes, lanes), x[l].reshape(nodes, 3 * lanes))
@@ -449,7 +510,8 @@
             sta_slots[me_sta] = chunk_of(w_local, me_sta)[...]
         for h in range(HALVES):
             own = slice(h * half, (h + 1) * half)
-            halo_wait(e, (1 - h,))
+            if e > top:
+                halo_wait(e, (1 - h,))
             mix_sta(1, e, h, xb)
             if l == 0 and h == 0:
                 for copy in first:
@@ -472,7 +534,8 @@
                     second[-1].start()
             early = xb[own, :, 0 : 2 * lanes].reshape(part_nodes, 2 * lanes)
             grad = grads[h] + dot(early, wf[1, l, 0 : 2 * lanes])
-            halo_wait(e, (2 + 2 * h, 3 + 2 * h))
+            if e > top:
+                halo_wait(e, (2 + 2 * h, 3 + 2 * h))
             mix_src(1, e, h, xb)
             late = xb[own, :, 2 * lanes :].reshape(part_nodes, lanes)
             grad = grad + dot(late, wf[1, l, 2 * lanes :])
@@ -503,8 +566,10 @@
         )
         third[-1].start()
     for e in range(2 * LAYERS):
-        halo_drain(e)
-    for copy in sends + first + second:
+        if e != top:
+            halo_drain(e)
+    tiles(lambda copy: copy.wait_send(), False)
+    for copy in first + second:
         copy.wait_send()
     for copy in third:
         copy.wait_recv()
@@ -602,8 +667,7 @@
             pltpu.VMEM((2, G * cols, G * span_r), BF16),
             pltpu.VMEM((2, LAYERS, 3 * lanes, lanes), BF16),
             pltpu.VMEM((jw, nodes), BF16),
-            pltpu.VMEM((nodes, jw), BF16),
-            pltpu.VMEM((n_sta, 8, lanes), F32),
+            pltpu.VMEM((3, n_sta, 8, lanes), F32),
             pltpu.VMEM((w_rows, lanes), F32),
             pltpu.VMEM((n_sta, chunk, lanes), F32),
             pltpu.VMEM((n_src, chunk, lanes), BF16),
@@ -612,8 +676,8 @@
             dma((HALVES + 2,)),
             dma((2 * LAYERS, 2 + 2 * HALVES)),
             dma((2 * LAYERS, 2 + 2 * HALVES)),
-            dma((n_sta,)),
-            dma((n_sta,)),
+            dma((3, n_sta)),
+            dma((3, n_sta)),
             dma((n_sta,)),
             dma((n_sta,)),
             dma((n_src,)),

time: 49.3 us -> 45 us (0.913)
  Pallas kernels: 48.5 us -> 44.2 us
    pallas_call x1, Pallas kernels: 46.1 us -> 41.8 us  [shards(): pl.pallas_call(functools.partial(kernel, n_sta, n_src, chunk), out_shape=...]
where the time goes in v5:
time: 45 us; the launch traced here: 44.8 us
  Pallas kernels  44.2 us (98%)
  between operations  0.64 us (1%)
    pallas_call x1, Pallas kernels, shards(): pl.pallas_call(functools.partial(kernel, n_sta, n_src, chunk), out_shape=...  41.8 us
    pallas_call x1, Pallas kernels, shards(): pl.pallas_call(functools.partial(finish, factor), out_shape=(jax.ShapeDty...  2.39 us

profile of v5, /device:TPU:0, one launch (start us, length us, event | category | flops | bytes accessed | tf_op | source)
XLA Modules:
  0.0 44.8 jit_solution(9183633137472028098)
XLA Ops:
  0.6 41.8 %shard_map.120 = (f32[2,32]{1,0:T(2,128)}, bf16[32,32,128]{2,1,0:T(8,128)(2,1)}, f32[256,128]{1,0:T(8,128)}) custom-call(bf16[32,32,128]{2,1,0:T(8,128)(2,1)} %feat.1, s32[16,128]{1,0:T(8,128)} %bitcast.7, s32[1,128]{1,0:T(1,128)} %bitcast.9, s32[16,256]{1,0:T(8,128)} %bitcast.6, s32[1,256]{1,0:T(1,128)} %bitcast.8, s32[2,32]{1,0:T(2,128)} %picks_hbm.1, ...), custom_call_target="tpu_custom_call" | custom-call | tf_op jit(solution)/shard_map/pallas_call | solution.py:648
  42.4 2.4 %shard_map.121 = (f32[2,32]{1,0:T(2,128)}, bf16[32,32,128]{2,1,0:T(8,128)(2,1)}, f32[2,3,64,64]{3,2,1,0:T(8,128)}, f32[1,64]{1,0:T(1,128)}) custom-call(f32[2,32]{1,0:T(2,128)} %get-tuple-element.11.lik, bf16[32,32,128]{2,1,0:T(8,128)(2,1)} %get-tuple-element.12.grad, f32[256,128]{1,0:T(8,128)} %get-tuple-element.13.w_sum), custom_call_target="tpu_custom_call" | custom-call | tf_op jit(solution)/shard_map/pallas_call | solution.py:693

commit v6 on v5

--- a/solution.py
+++ b/solution.py
@@ -461,17 +461,22 @@
         spots = range(h * half, (h + 1) * half)
         grads.append(jnp.concatenate([err_own * picks_own[i : i + 1] for i in spots], axis=0))
         put_delta(LAYERS - 1, h, grads[h])
-    for m in range(HW):
-        up = picks_up[rows - HW + m : rows - HW + m + 1]
-        hs[top, m] = scaled(hs[top, m], err_own, up)
-        hs[top, HW + rows + m] = scaled(hs[top, HW + rows + m], err_own, picks_down[m : m + 1])
-    for i in range(rows):
-        own_row = picks_own[i : i + 1]
-        hr[top, i, 0:HW] = scaled(hr[top, i, 0:HW], err_left, own_row)
-        hr[top, i, HW + cols :] = scaled(hr[top, i, HW + cols :], err_right, own_row)
+    def rim_deltas(h):
+        for m in range(HW):
+            if h == 0:
+                up = picks_up[rows - HW + m : rows - HW + m + 1]
+                hs[top, m] = scaled(hs[top, m], err_own, up)
+            else:
+                down = picks_down[m : m + 1]
+                hs[top, HW + rows + m] = scaled(hs[top, HW + rows + m], err_own, down)
+        for i in range(h * half, (h + 1) * half):
+            own_row = picks_own[i : i + 1]
+            hr[top, i, 0:HW] = scaled(hr[top, i, 0:HW], err_left, own_row)
+            hr[top, i, HW + cols :] = scaled(hr[top, i, HW + cols :], err_right, own_row)
 
     def weight_sums(l):
-        w_t = dot_tn(xb[:, :, 0:lanes].reshape(nodes, lanes), x[l].reshape(nodes, 3 * lanes))
+        delta = hs[2 * LAYERS - 1 - l, HW : HW + rows].reshape(nodes, lanes)
+        w_t = dot_tn(delta, x[l].reshape(nodes, 3 * lanes))
         folded = []
         for p in range(3):
             both = jnp.where(
@@ -490,9 +495,8 @@
     first, second, third = [], [], []
     for l in reversed(range(LAYERS)):
         e = 2 * LAYERS - 1 - l
-        if l == 1:
-            kept = weight_sums(l)
-        else:
+        if l == 0:
+            kept = weight_sums(1)
             w_local[2 * feature : 3 * feature] = jnp.where(first_window, weight_sums(l), kept)
             w_local[3 * feature :] = jnp.broadcast_to(v_row, (w_local.shape[0] - 3 * feature, lanes))
             for d in range(1, n_sta):
@@ -512,6 +516,8 @@
             own = slice(h * half, (h + 1) * half)
             if e > top:
                 halo_wait(e, (1 - h,))
+            else:
+                rim_deltas(h)
             mix_sta(1, e, h, xb)
             if l == 0 and h == 0:
                 for copy in first:

time: 45 us -> 44.7 us (level)
  no operation moved by 1% of the time
where the time goes in v6:
time: 44.7 us; the launch traced here: 44.5 us
  Pallas kernels  43.8 us (98%)
  between operations  0.64 us (1%)
    pallas_call x1, Pallas kernels, shards(): pl.pallas_call(functools.partial(kernel, n_sta, n_src, chunk), out_shape=...  41.4 us
    pallas_call x1, Pallas kernels, shards(): pl.pallas_call(functools.partial(finish, factor), out_shape=(jax.ShapeDty...  2.39 us

profile of v6, /device:TPU:0, one launch (start us, length us, event | category | flops | bytes accessed | tf_op | source)
XLA Modules:
  0.0 44.5 jit_solution(15579812677111441263)
XLA Ops:
  0.6 41.4 %shard_map.120 = (f32[2,32]{1,0:T(2,128)}, bf16[32,32,128]{2,1,0:T(8,128)(2,1)}, f32[256,128]{1,0:T(8,128)}) custom-call(bf16[32,32,128]{2,1,0:T(8,128)(2,1)} %feat.1, s32[16,128]{1,0:T(8,128)} %bitcast.7, s32[1,128]{1,0:T(1,128)} %bitcast.9, s32[16,256]{1,0:T(8,128)} %bitcast.6, s32[1,256]{1,0:T(1,128)} %bitcast.8, s32[2,32]{1,0:T(2,128)} %picks_hbm.1, ...), custom_call_target="tpu_custom_call" | custom-call | tf_op jit(solution)/shard_map/pallas_call | solution.py:654
  42.1 2.4 %shard_map.121 = (f32[2,32]{1,0:T(2,128)}, bf16[32,32,128]{2,1,0:T(8,128)(2,1)}, f32[2,3,64,64]{3,2,1,0:T(8,128)}, f32[1,64]{1,0:T(1,128)}) custom-call(f32[2,32]{1,0:T(2,128)} %get-tuple-element.11.lik, bf16[32,32,128]{2,1,0:T(8,128)(2,1)} %get-tuple-element.12.grad, f32[256,128]{1,0:T(8,128)} %get-tuple-element.13.w_sum), custom_call_target="tpu_custom_call" | custom-call | tf_op jit(solution)/shard_map/pallas_call | solution.py:699
